TPU v7x, 256 devices: a whole 4x4x8 slice. The times are simulated.
256 devices in a mesh: gx: 8 (over y, z_lo), gy: 8 (over x, core), gz: 4 (over z_hi).
Axes of the slice: x: 4, y: 4, z: 8 (z_hi: 4, z_lo: 2; z = z_hi * 2 + z_lo), core: 2. Of those that a mesh axis runs over, the one named last changes fastest.
Arguments:
- tokens: bfloat16 [512, 12288], P(('gx', 'gz'), 'gy'), may hold values from -6 to 6
- w_in: bfloat16 [12288, 49152], P('gy', ('gx', 'gz')), may hold values from -0.0546875 to 0.0546875
- bias: float32 [49152], P(('gx', 'gz')), may hold values from -4 to 4
- grad_act: bfloat16 [512, 49152], P('gy', ('gx', 'gz')), may hold values from -6 to 6
Outputs:
- act: bfloat16 [512, 49152], P('gy', ('gx', 'gz'))
- grad_bias: float32 [49152], P(('gx', 'gz'))
- grad_weight: bfloat16 [12288, 49152], P('gy', ('gx', 'gz'))
- grad_tokens: bfloat16 [512, 12288], P(('gx', 'gz'), 'gy')
All inputs are finite; a program needn't handle non-finite values.
Results may differ from a plain program's by a relative error of at most 0.007.
Values may be sent and summed in bfloat16 or wider, within the bound.
No kernel may reach another device: no remote copies, remote signals or barrier semaphores. Data moves between devices by JAX's collectives and lax.ppermute only.
A program may use at most 64 MiB of HBM per device.

v0:
```python
import math

import jax
import jax.numpy as jnp
from jax import lax
from jax.sharding import PartitionSpec as P


def gelu_pair(v):
    coef = math.sqrt(2.0 / math.pi)
    tangent = jnp.tanh(coef * (v + 0.044715 * v * v * v))
    value = 0.5 * v * (1.0 + tangent)
    slope = 0.5 * (1.0 + tangent) + 0.5 * v * (1.0 - tangent * tangent) * coef * (
        1.0 + 3.0 * 0.044715 * v * v
    )
    return (value, slope)


def on_device(tokens, w_in, bias, grad_act):
    gathered = lax.all_gather(tokens, ("gx", "gz"), axis=0, tiled=True)
    block = gathered
    preact = (
        lax.psum_scatter(
            jnp.dot(block, w_in, preferred_element_type=jnp.float32),
            "gy",
            scatter_dimension=0,
            tiled=True,
        )
        + bias
    )
    value, slope = gelu_pair(preact)
    act = value.astype(jnp.bfloat16)
    grad_pre = (grad_act.astype(jnp.float32) * slope).astype(jnp.bfloat16)
    piece = lax.all_gather(grad_pre, "gy", axis=0, tiled=True)
    block = gathered
    weight_sum = lax.dot_general(
        block, piece, (((0,), (0,)), ((), ())), preferred_element_type=jnp.float32
    )
    weight_sum, grad_full = (weight_sum, piece)
    grad_weight = weight_sum.astype(jnp.bfloat16)
    grad_bias = lax.psum(jnp.sum(grad_pre, axis=0, dtype=jnp.float32), "gy")
    block = grad_full
    grad_tokens = lax.psum_scatter(
        lax.dot_general(block, w_in, (((1,), (1,)), ((), ())), preferred_element_type=jnp.float32),
        ("gx", "gz"),
        scatter_dimension=0,
        tiled=True,
    ).astype(jnp.bfloat16)
    return (act, grad_bias, grad_weight, grad_tokens)


def solution(mesh):
    placed = (P(("gx", "gz"), "gy"), P("gy", ("gx", "gz")), P(("gx", "gz")), P("gy", ("gx", "gz")))
    return jax.shard_map(
        on_device,
        mesh=mesh,
        in_specs=placed,
        out_specs=(
            P("gy", ("gx", "gz")),
            P(("gx", "gz")),
            P("gy", ("gx", "gz")),
            P(("gx", "gz"), "gy"),
        ),
        check_vma=False,
    )
```

profile of v0, /device:TPU:32, one launch (start us, length us, event | category | flops | bytes accessed | tf_op | source)
XLA Modules:
  0.0 397.1 jit_solution(6037731921537123118)
XLA Ops:
  7.2 0.0 all-gather.3.cloned.1.call-start
  7.2 0.7 all-gather.3.cloned.1.call-update
  7.9 0.0 reduce-scatter.3.cloned.1.call-start
  7.9 147.7 %all-gather.3.cloned.1.call-done = bf16[512,1536]{1,0:T(8,128)(2,1)} async-done(((bf16[16,1536]{1,0:T(8,128)(2,1)}), bf16[512,1536]{1,0:T(8,128)(2,1)}) %all-gather.3.cloned.1.call-update) | async-done | bytes 1572880 | tf_op jit(solution)/shard_map/all_gather | solution.py:20
  155.6 7.1 %fusion.9 = f32[512,1536]{1,0:T(8,128)} fusion(bf16[512,1536]{1,0:T(8,128)(2,1)} %all-gather.3.cloned.1.call-done, bf16[1536,1536]{1,0:T(8,128)(2,1)} %param.5), kind=kOutput, calls=%fused_computation.13 | convolution fusion | flops 2415919104 | bytes 9437184 | tf_op jit(solution)/shard_map/dot_general | solution.py:24
  162.7 0.0 copy-start
  162.7 0.0 reduce-scatter.3.cloned.1.call-update
  162.7 0.0 all-gather.5.cloned.1.call-start
  162.8 37.2 %reduce-scatter.3.cloned.1.call-done = f32[64,1536]{1,0:T(8,128)} async-done(((f32[512,1536]{1,0:T(8,128)}), f32[64,1536]{1,0:T(8,128)}) %reduce-scatter.3.cloned.1.call-update) | async-done | bytes 393232 | tf_op jit(solution)/shard_map/reduce_scatter | solution.py:23
  199.9 0.0 copy-done
  199.9 0.0 copy-done.1
  199.9 2.0 convert_reduce_fusion
  202.0 0.0 all-gather.5.cloned.1.call-update
  202.0 0.0 reduce-scatter.5.cloned.1.call-start
  202.1 26.2 %all-gather.5.cloned.1.call-done = bf16[512,1536]{1,0:T(8,128)(2,1)} async-done(((bf16[64,1536]{1,0:T(8,128)(2,1)}), bf16[512,1536]{1,0:T(8,128)(2,1)}) %all-gather.5.cloned.1.call-update) | async-done | bytes 1572880 | tf_op jit(solution)/shard_map/all_gather | solution.py:34
  228.3 7.1 %fusion.10 = f32[512,1536]{1,0:T(8,128)} fusion(bf16[512,1536]{1,0:T(8,128)(2,1)} %all-gather.5.cloned.1.call-done, bf16[1536,1536]{1,0:T(8,128)(2,1)} %param.5), kind=kOutput, calls=%fused_computation.14 | convolution fusion | flops 2415919104 | bytes 9437184 | tf_op jit(solution)/shard_map/dot_general | solution.py:44
  235.4 0.0 reduce-scatter.5.cloned.1.call-update
  235.4 14.4 %psum.7 = f32[1536]{0:T(1024)} all-reduce(f32[1536]{0:T(1024)S(1)} %get-tuple-element.8), channel_id=1, replica_groups=mesh['gx'=8,'gy'=8,'gz'=4] {'gy'}, use_global_device_ids=true, to_apply=%region_2.0 | all-reduce | flops 1536 | bytes 12288 | tf_op jit(solution)/shard_map/psum | solution.py:41
  249.8 0.0 copy-done.2
  249.8 0.0 copy-done.3
  249.8 4.4 %fusion = bf16[1536,1536]{0,1:T(8,128)(2,1)} fusion(bf16[512,1536]{1,0:T(8,128)(2,1)S(1)} %copy-done.3, bf16[512,1536]{1,0:T(8,128)(2,1)S(1)} %copy-done.2), kind=kOutput, calls=%fused_computation.1 | convolution fusion | flops 2418278400 | bytes 7864320 | tf_op jit(solution)/shard_map/dot_general | solution.py:36
  254.2 6.6 %copy.8 = bf16[1536,1536]{1,0:T(8,128)(2,1)} copy(bf16[1536,1536]{0,1:T(8,128)(2,1)} %fusion) | data formatting | bytes 9437184
  260.8 128.3 %reduce-scatter.5.cloned.1.call-done = f32[16,1536]{1,0:T(8,128)} async-done(((f32[512,1536]{1,0:T(8,128)}), f32[16,1536]{1,0:T(8,128)}) %reduce-scatter.5.cloned.1.call-update) | async-done | bytes 98320 | tf_op jit(solution)/shard_map/reduce_scatter | solution.py:43
  389.1 1.5 convert_element_type.27
  (3 shorter events, 0.0 us)
Async XLA Ops:
  7.2 148.4 %all-gather.3.cloned.1.call-start = ((), (), s32[]{:S(2)}) async-start(), calls=%async_computation.2 | async-start | bytes 1622016 | tf_op jit(solution)/shard_map/all_gather | solution.py:20
  7.9 192.0 %reduce-scatter.3.cloned.1.call-start = ((), (), s32[]{:S(2)}) async-start(), calls=%async_computation.3 | async-start | bytes 3538944 | tf_op jit(solution)/shard_map/reduce_scatter | solution.py:23
  162.7 37.2 %copy-start = (bf16[64,1536]{1,0:T(8,128)(2,1)S(1)}, bf16[64,1536]{1,0:T(8,128)(2,1)}, u32[]{:S(2)}) copy-start(bf16[64,1536]{1,0:T(8,128)(2,1)} %param.7) | copy-start | bytes 589828
  162.7 37.2 %copy-start.1 = (f32[1536]{0:T(1024)S(1)}, f32[1536]{0:T(1024)}, u32[]{:S(2)}) copy-start(f32[1536]{0:T(1024)} %param.6) | copy-start | bytes 18436
  162.7 65.6 %all-gather.5.cloned.1.call-start = ((), (), s32[]{:S(2)}) async-start(), calls=%async_computation.4 | async-start | bytes 1769472 | tf_op jit(solution)/shard_map/all_gather | solution.py:34
  202.0 187.1 %reduce-scatter.5.cloned.1.call-start = ((), (), s32[]{:S(2)}) async-start(), calls=%async_computation.5 | async-start | bytes 3244032 | tf_op jit(solution)/shard_map/reduce_scatter | solution.py:43
  235.4 14.4 %copy-start.2 = (bf16[512,1536]{1,0:T(8,128)(2,1)S(1)}, bf16[512,1536]{1,0:T(8,128)(2,1)}, u32[]{:S(2)}) copy-start(bf16[512,1536]{1,0:T(8,128)(2,1)} %all-gather.3.cloned.1.call-done) | copy-start | bytes 4718596
  235.4 14.4 %copy-start.3 = (bf16[512,1536]{1,0:T(8,128)(2,1)S(1)}, bf16[512,1536]{1,0:T(8,128)(2,1)}, u32[]{:S(2)}) copy-start(bf16[512,1536]{1,0:T(8,128)(2,1)} %all-gather.5.cloned.1.call-done) | copy-start | bytes 4718596
Sparse Core Ops, SparseCore 0:
  9.8 145.7 all-gather.2
  162.8 37.0 reduce-scatter.2
  202.3 25.8 all-gather.4
  235.5 153.5 reduce-scatter.4
where the time goes:
time: 402 us; the launch traced here: 397 us
  waiting for transfers between devices  340 us (85%)
  matrix products  18.5 us (5%)
  blocking collectives  14.4 us (4%)
  between operations  13.8 us (3%)
  local copies, waits for them, and re-layouts  6.64 us (2%)
    all_gather x1, waiting for transfers between devices, on_device(): gathered = lax.all_gather(tokens, ('gx', 'gz'), axis=0, tiled=True)  148 us
    reduce_scatter x1, waiting for transfers between devices, on_device(): lax.psum_scatter(lax.dot_general(block, w_in, (((1,), (1,)), ((), ())), p...  128 us
    reduce_scatter x1, waiting for transfers between devices, on_device(): lax.psum_scatter(jnp.dot(block, w_in, preferred_element_type=jnp.float32)...  37.2 us
    all_gather x1, waiting for transfers between devices, on_device(): piece = lax.all_gather(grad_pre, 'gy', axis=0, tiled=True)  26.2 us
    psum x1, blocking collectives, on_device(): grad_bias = lax.psum(jnp.sum(grad_pre, axis=0, dtype=jnp.float32), 'gy')  14.4 us
  transfers between devices with their start and end apart: 4, of which 4 were waited for; matrix products, arithmetic and copies ran while one was open for 3% of the time, Pallas kernels for 0%

commit v1 on v0

v1 whole, which is shorter than its diff:
```python
import functools
import math

import jax
import jax.numpy as jnp
from jax import lax
from jax.experimental import pallas as pl
from jax.experimental.pallas import tpu as pltpu
from jax.sharding import PartitionSpec as P

EVEN = ((0, 2, 4, 6),)
ODD = ((1, 3, 5, 7),)
BF = jnp.bfloat16
F32 = jnp.float32
ROW = 16
VMEM = pltpu.VMEM
LIMIT = 48 * 1024 * 1024
PLANE = ("gx", "gz")


def flat(y, z):
    return (y % 4 * 2 + z % 2) * 4 + z % 8 // 2


def by_plane(array, dy, dz):
    pairs = [(flat(y, z), flat(y + dy, z + dz)) for y in range(4) for z in range(8)]
    return lax.ppermute(array, PLANE, pairs)


def by_line(array, dx, flip=0):
    pairs = [(2 * x + c, (x + dx) % 4 * 2 + (c ^ flip)) for x in range(4) for c in range(2)]
    return lax.ppermute(array, "gy", pairs)


def call(body, ins, outs, grid=(), scratch=(), flops=0, moved=0):
    whole = lambda shape: pl.BlockSpec(shape, lambda *_: (0,) * len(shape))
    in_specs = [s if s is not None else whole(a.shape) for a, s in ins]
    out_specs = [s if s is not None else whole(shape) for shape, _, s in outs]
    return pl.pallas_call(
        body,
        grid=grid or (1,),
        in_specs=in_specs,
        out_specs=out_specs,
        out_shape=[jax.ShapeDtypeStruct(shape, kind) for shape, kind, _ in outs],
        scratch_shapes=list(scratch),
        compiler_params=pltpu.CompilerParams(vmem_limit_bytes=LIMIT),
        cost_estimate=pl.CostEstimate(flops=flops, bytes_accessed=moved, transcendentals=0),
    )(*[a for a, _ in ins])


SMEM = pl.BlockSpec(memory_space=pltpu.SMEM)


def project(place, blocks, w_in, tile=512):
    half = blocks[0].shape[0] // 2
    depth, width = w_in.shape
    rows = 8 * half

    def body(place, b0, b1, b2, b3, w, held, keep, give):
        x, c, y, l = (place[i] for i in range(4))

        @pl.when(pl.program_id(0) == 0)
        def _():
            for t, block in enumerate((b0, b1, b2, b3)):
                at = (y + t - x + 4) % 4
                for p in range(2):
                    side = (l + p + c) % 2
                    held[side, at] = block[p * half : (p + 1) * half, :]

        found = jnp.dot(held[...].reshape(rows, depth), w[...], preferred_element_type=F32)
        keep[...] = found[: rows // 2].reshape(keep.shape)
        give[...] = found[rows // 2 :].reshape(give.shape).astype(BF)

    return call(
        body,
        [(place, SMEM)]
        + [(b, None) for b in blocks]
        + [(w_in, pl.BlockSpec((depth, tile), lambda j: (0, j)))],
        [
            ((2, 4, half, depth), BF, None),
            ((4, half, width), F32, pl.BlockSpec((4, half, tile), lambda j: (0, 0, j))),
            ((4, half, width), BF, pl.BlockSpec((4, half, tile), lambda j: (0, 0, j))),
        ],
        grid=(width // tile,),
        flops=2 * rows * depth * width,
        moved=2 * depth * width + 5 * rows * width,
    )


def add_pair(keep, got):
    _, half, width = keep.shape

    def body(keep, got, own, *rest):
        own[...] = keep[0] + got[0].astype(F32)
        for d, out in enumerate(rest, 1):
            out[...] = (keep[d] + got[d].astype(F32)).astype(BF)

    return call(
        body,
        [(keep, None), (got, None)],
        [((half, width), F32, None)] + [((half, width), BF, None)] * 3,
        flops=keep.size,
        moved=8 * keep.size,
    )


def bend(place, own, parts, bias, grad_act, even, odd):
    half, width = own.shape
    coef = math.sqrt(2.0 / math.pi)

    def body(place, own, p1, p2, p3, bias, grad_act, act, grad):
        c, l, h = place[1], place[3], place[4]
        odd_turn = (c + l) % 2
        for j in range(half // ROW):
            here = slice(j * ROW, (j + 1) * ROW)
            step = jnp.where(odd_turn == 1, odd[j], even[j])
            at = (2 * h + l + step) % 8 // 2
            v = own[here, :] + p1[here, :].astype(F32)
            v = v + (p2[here, :].astype(F32) + p3[here, :].astype(F32)) + bias[...]
            t = jnp.tanh(coef * (v + 0.044715 * v * v * v))
            act[here, :] = (0.5 * v * (1.0 + t)).astype(BF)
            slope = 0.5 * (1.0 + t) + 0.5 * v * (1.0 - t * t) * coef * (1.0 + 3.0 * 0.044715 * v * v)
            grad[here, :] = (grad_act[at].astype(F32) * slope).astype(BF)

    return call(
        body,
        [(place, SMEM), (own, None)] + [(p, None) for p in parts] + [(bias, None), (grad_act, None)],
        [((half, width), BF, None)] * 2,
        flops=30 * own.size,
        moved=14 * own.size,
    )


def back(place, mine, other, w_in, tile=512):
    _, half, width = mine.shape
    depth = w_in.shape[0]
    rows = 8 * half

    def body(place, mine, other, w, o0, o1, o2, o3, found):
        x, c, y, l = (place[i] for i in range(4))
        turn = (((1,), (1,)), ((), ()))
        for side, part in enumerate((mine, other)):
            part = part[...].reshape(4 * half, width)
            product = lax.dot_general(part, w[...], turn, preferred_element_type=F32)
            found[side] = product.reshape(4, half, tile)
        for t, out in enumerate((o0, o1, o2, o3)):
            at = (y + t - x + 4) % 4
            for p in range(2):
                side = (l + p + c) % 2
                out[p * half : (p + 1) * half, :] = found[side, at].astype(out.dtype)

    return call(
        body,
        [(place, SMEM), (mine, None), (other, None)]
        + [(w_in, pl.BlockSpec((tile, width), lambda j: (j, 0)))],
        [
            ((2 * half, depth), F32 if t == 0 else BF, pl.BlockSpec((2 * half, tile), lambda j: (0, j)))
            for t in range(4)
        ],
        grid=(depth // tile,),
        scratch=[VMEM((2, 4, half, tile), F32)],
        flops=2 * rows * depth * width,
        moved=2 * depth * width + 4 * rows * width,
    )


def add_four(own, parts, steps):
    rows, width = own.shape

    def body(own, p1, p2, p3, *outs):
        for j, out in enumerate(outs):
            here = slice(j * ROW, (j + 1) * ROW)
            v = own[here, :] + p1[here, :].astype(F32)
            v = v + (p2[here, :].astype(F32) + p3[here, :].astype(F32))
            out[...] = v.astype(out.dtype)

    return call(
        body,
        [(own, None)] + [(p, None) for p in parts],
        [((ROW, width), F32 if s == 0 else BF, None) for s in steps],
        flops=3 * own.size,
        moved=12 * own.size,
    )


def add_all(arrays):
    def body(*refs):
        total = refs[0][...].astype(F32)
        for ref in refs[1:-1]:
            total = total + ref[...].astype(F32)
        refs[-1][...] = total.astype(BF)

    shape = arrays[0].shape
    return call(
        body,
        [(a, None) for a in arrays],
        [(shape, BF, None)],
        flops=8 * arrays[0].size,
        moved=18 * arrays[0].size,
    )[0]


def weigh(place, held, mine, other, acts, tile=256):
    chunks = len(held)
    half, depth = held[0].shape[2:]
    width = mine[0].shape[2]
    rows = 4 * half

    def body(place, *refs):
        held, refs = refs[:chunks], refs[chunks:]
        mine, refs = refs[:chunks], refs[chunks:]
        other, refs = refs[:chunks], refs[chunks:]
        acts, refs = refs[:chunks], refs[chunks:]
        weight, bias, act = refs

        @pl.when(pl.program_id(0) == 0)
        def _():
            total = jnp.zeros((1, width), F32)
            for ref in mine + other:
                part = ref[...].reshape(rows, width).astype(F32)
                total = total + jnp.sum(part, axis=0, keepdims=True)
            bias[...] = total
            c, l, h = place[1], place[3], place[4]
            odd_turn = (c + l) % 2
            for k in range(chunks):
                for j in range(half // ROW):
                    step = jnp.where(odd_turn == 1, ODD[k][j], EVEN[k][j])
                    at = (2 * h + l + step) % 8 // 2
                    act[at] = acts[k][j * ROW : (j + 1) * ROW, :]

        total = None
        for k in range(chunks):
            for side, part in enumerate((mine[k], other[k])):
                product = lax.dot_general(
                    held[k][side].reshape(rows, tile),
                    part[...].reshape(rows, width),
                    (((0,), (0,)), ((), ())),
                    preferred_element_type=F32,
                )
                total = product if total is None else total + product
        weight[...] = total.astype(BF)

    return call(
        body,
        [(place, SMEM)]
        + [(a, pl.BlockSpec((2, 4, half, tile), lambda j: (0, 0, 0, j))) for a in held]
        + [(a, None) for a in (*mine, *other, *acts)],
        [
            ((depth, width), BF, pl.BlockSpec((tile, width), lambda j: (j, 0))),
            ((1, width), F32, None),
            ((4, ROW, width), BF, None),
        ],
        grid=(depth // tile,),
        flops=4 * chunks * rows * depth * width,
        moved=2 * depth * width + 8 * chunks * rows * width,
    )


def on_device(tokens, w_in, bias, grad_act):
    gx, gy, gz = (lax.axis_index(a) for a in ("gx", "gy", "gz"))
    place = jnp.stack([gy // 2, gy % 2, gx // 2, gx % 2, gz]).astype(jnp.int32)
    width = w_in.shape[1]
    bias = bias.reshape(1, width)
    grad_act = grad_act.reshape(4, ROW, width)
    chunks = range(len(EVEN))

    with jax.named_scope("gather_z"):
        far = {0: tokens}
        for k in chunks:
            for s in EVEN[k] + ODD[k]:
                if s:
                    far[s] = by_plane(tokens, 0, -s)
    blocks = []
    for k in chunks:
        with jax.named_scope("gather_y"):
            own = jnp.concatenate([far[s] for s in EVEN[k] + ODD[k]], axis=0)
            blocks.append([own] + [by_plane(own, -t, 0) for t in (1, 2, 3)])
    held, acts, mine, other, ends = [], [], [], [], {}
    for k in chunks:
        with jax.named_scope("project"):
            order, keep, give = project(place, blocks[k], w_in)
            held.append(order)
        with jax.named_scope("reduce_x"):
            own, *parts = add_pair(keep, by_line(give, 0, 1))
            parts = [by_line(p, d) for d, p in enumerate(parts, 1)]
        with jax.named_scope("bend"):
            act, grad = bend(place, own, parts, bias, grad_act, EVEN[k], ODD[k])
            acts.append(act)
        with jax.named_scope("gather_x"):
            grads = jnp.stack([grad] + [by_line(grad, -d) for d in (1, 2, 3)])
            mine.append(grads)
            other.append(by_line(grads, 0, 1))
    for k in chunks:
        with jax.named_scope("back"):
            own, *parts = back(place, mine[k], other[k], w_in)
        with jax.named_scope("reduce_y"):
            parts = [by_plane(p, t, 0) for t, p in enumerate(parts, 1)]
            steps = EVEN[k] + ODD[k]
            sums = add_four(own, parts, steps)
        with jax.named_scope("reduce_z"):
            for s, part in zip(steps, sums):
                ends[s] = by_plane(part, 0, s) if s else part
    with jax.named_scope("weigh"):
        grad_weight, grad_bias, act = weigh(place, held, mine, other, acts)
    with jax.named_scope("finish"):
        grad_tokens = add_all([ends[s] for s in range(8)])
    return (act.reshape(4 * ROW, width), grad_bias.reshape(width), grad_weight, grad_tokens)


def solution(mesh):
    placed = (P(("gx", "gz"), "gy"), P("gy", ("gx", "gz")), P(("gx", "gz")), P("gy", ("gx", "gz")))
    return jax.shard_map(
        on_device,
        mesh=mesh,
        in_specs=placed,
        out_specs=(
            P("gy", ("gx", "gz")),
            P(("gx", "gz")),
            P("gy", ("gx", "gz")),
            P(("gx", "gz"), "gy"),
        ),
        check_vma=False,
    )
```

time: 402 us -> 136 us (0.34)
  waiting for transfers between devices: 340 us -> 58.6 us
  starting transfers between devices: 0.16 us -> 54.4 us
  matrix products: 18.5 us -> 0 us
  Pallas kernels: 0 us -> 18.1 us
  blocking collectives: 14.4 us -> 0 us
  between operations: 13.8 us -> 0.78 us
  local copies, waits for them, and re-layouts: 6.64 us -> 0.97 us
    all_gather x2 -> x0, waiting for transfers between devices: 174 us -> none  [the longest x1 148 us: on_device(): gathered = lax.all_gather(tokens, ('gx', 'gz'), axis=0, tiled=True)]
    reduce_scatter x2 -> x0, waiting for transfers between devices: 165 us -> none  [the longest x1 128 us: on_device(): lax.psum_scatter(lax.dot_general(block, w_in, (((1,), (1,)), ((), ())), p...]
    ppermute x0 -> x28, waiting for transfers between devices: none -> 58.6 us  [the longest x20 39 us: by_plane(): return lax.ppermute(array, PLANE, pairs)]
    ppermute x0 -> x28, starting transfers between devices: none -> 54.4 us  [the longest x20 43.1 us: by_plane(): return lax.ppermute(array, PLANE, pairs)]
    dot_general x3 -> x0, matrix products: 18.5 us -> none  [the longest x1 7.1 us: on_device(): lax.dot_general(block, w_in, (((1,), (1,)), ((), ())), preferred_element_...]
    pallas_call x0 -> x7, Pallas kernels: none -> 18.1 us  [call(): pl.pallas_call(body, grid=grid or (1,), in_specs=in_specs, out_specs=out_...]
    psum x1 -> x0, blocking collectives: 14.4 us -> none  [on_device(): grad_bias = lax.psum(jnp.sum(grad_pre, axis=0, dtype=jnp.float32), 'gy')]
    unnamed x9 -> x11, local copies, waits for them, and re-layouts: 6.64 us -> 0.87 us
  transfers between devices with their start and end apart: 4 -> 28, of which waited for: 4 -> 14; matrix products, arithmetic and copies ran while one was open for 3% -> 1% of each run, Pallas kernels for 0% -> 4%
where the time goes in v1:
time: 136 us; the launch traced here: 134 us
  waiting for transfers between devices  58.6 us (43%)
  starting transfers between devices  54.4 us (40%)
  Pallas kernels  18.1 us (13%)
    ppermute x20, starting transfers between devices, by_plane(): return lax.ppermute(array, PLANE, pairs)  43.1 us
    ppermute x20, waiting for transfers between devices, by_plane(): return lax.ppermute(array, PLANE, pairs)  39 us
    ppermute x8, waiting for transfers between devices, by_line(): return lax.ppermute(array, 'gy', pairs)  19.7 us
    pallas_call x7, Pallas kernels, call(): pl.pallas_call(body, grid=grid or (1,), in_specs=in_specs, out_specs=out_...  18.1 us
    ppermute x8, starting transfers between devices, by_line(): return lax.ppermute(array, 'gy', pairs)  11.3 us
  transfers between devices with their start and end apart: 28, of which 14 were waited for; matrix products, arithmetic and copies ran while one was open for 1% of the time, Pallas kernels for 4%

profile of v1, /device:TPU:32, one launch (start us, length us, event | category | flops | bytes accessed | tf_op | source)
XLA Modules:
  0.0 133.5 jit_solution(4187428764754505458)
XLA Ops:
  0.6 5.9 %collective-permute-start.5 = (bf16[16,1536]{1,0:T(8,128)(2,1)}, bf16[16,1536]{1,0:T(8,128)(2,1)S(1)}, u32[]{:S(2)}, u32[]{:S(2)}) collective-permute-start(bf16[16,1536]{1,0:T(8,128)(2,1)} %param.4), channel_id=1, source_target_pairs={{0,33},{32,2},{1,34},{33,3},{2,35},{34,0},{3,32},{35,1},{64,97},{9... | collective-permute-start | bytes 147464 | tf_op jit(solution)/shard_map/gather_z/ppermute | solution.py:27
  9.1 3.0 %collective-permute-start = (bf16[16,1536]{1,0:T(8,128)(2,1)}, bf16[16,1536]{1,0:T(8,128)(2,1)S(1)}, u32[]{:S(2)}, u32[]{:S(2)}) collective-permute-start(bf16[16,1536]{1,0:T(8,128)(2,1)} %param.4), channel_id=1, source_target_pairs={{0,3},{32,35},{1,0},{33,32},{2,1},{34,33},{3,2},{35,34},{64,67},{9... | collective-permute-start | bytes 147464 | tf_op jit(solution)/shard_map/gather_z/ppermute | solution.py:27
  13.0 3.3 %collective-permute-done = bf16[16,1536]{1,0:T(8,128)(2,1)S(1)} collective-permute-done((bf16[16,1536]{1,0:T(8,128)(2,1)}, bf16[16,1536]{1,0:T(8,128)(2,1)S(1)}, u32[]{:S(2)}, u32[]{:S(2)}) %collective-permute-start) | collective-permute-done | bytes 49184 | tf_op jit(solution)/shard_map/gather_z/ppermute | solution.py:27
  16.2 3.7 %collective-permute-start.1 = (bf16[16,1536]{1,0:T(8,128)(2,1)}, bf16[16,1536]{1,0:T(8,128)(2,1)S(1)}, u32[]{:S(2)}, u32[]{:S(2)}) collective-permute-start(bf16[16,1536]{1,0:T(8,128)(2,1)} %param.4), channel_id=1, source_target_pairs={{0,2},{32,34},{1,3},{33,35},{2,0},{34,32},{3,1},{35,33},{64,66},{9... | collective-permute-start | bytes 147464 | tf_op jit(solution)/shard_map/gather_z/ppermute | solution.py:27
  19.9 5.1 %collective-permute-done.1 = bf16[16,1536]{1,0:T(8,128)(2,1)S(1)} collective-permute-done((bf16[16,1536]{1,0:T(8,128)(2,1)}, bf16[16,1536]{1,0:T(8,128)(2,1)S(1)}, u32[]{:S(2)}, u32[]{:S(2)}) %collective-permute-start.1) | collective-permute-done | bytes 49184 | tf_op jit(solution)/shard_map/gather_z/ppermute | solution.py:27
  27.0 2.3 %collective-permute-done.6 = bf16[16,1536]{1,0:T(8,128)(2,1)S(1)} collective-permute-done((bf16[16,1536]{1,0:T(8,128)(2,1)}, bf16[16,1536]{1,0:T(8,128)(2,1)S(1)}, u32[]{:S(2)}, u32[]{:S(2)}) %collective-permute-start.6) | collective-permute-done | bytes 49184 | tf_op jit(solution)/shard_map/gather_z/ppermute | solution.py:27
  30.9 2.9 %collective-permute-start.8 = (bf16[128,1536]{1,0:T(8,128)(2,1)S(1)}, bf16[128,1536]{1,0:T(8,128)(2,1)S(1)}, u32[]{:S(2)}, u32[]{:S(2)}) collective-permute-start(bf16[128,1536]{1,0:T(8,128)(2,1)S(1)} %constant_dynamic-update-slice_fusion.b0), channel_id=1, source_target_pairs={{0,128},{32,160},{1,129},{33,161},{2,130},{34,162},{3,131},{35,163... | collective-permute-start | bytes 1179656 | tf_op jit(solution)/shard_map/gather_y/ppermute | solution.py:27
  35.2 7.3 %collective-permute-done.9.b3 = bf16[128,1536]{1,0:T(8,128)(2,1)S(1)} collective-permute-done((bf16[128,1536]{1,0:T(8,128)(2,1)S(1)}, bf16[128,1536]{1,0:T(8,128)(2,1)S(1)}, u32[]{:S(2)}, u32[]{:S(2)}) %collective-permute-start.9) | collective-permute-done | bytes 393248 | tf_op jit(solution)/shard_map/gather_y/ppermute | solution.py:27
  42.5 4.8 %collective-permute-done.8.b2 = bf16[128,1536]{1,0:T(8,128)(2,1)S(1)} collective-permute-done((bf16[128,1536]{1,0:T(8,128)(2,1)S(1)}, bf16[128,1536]{1,0:T(8,128)(2,1)S(1)}, u32[]{:S(2)}, u32[]{:S(2)}) %collective-permute-start.8) | collective-permute-done | bytes 393248 | tf_op jit(solution)/shard_map/gather_y/ppermute | solution.py:27
  47.3 5.0 %project.1 = (bf16[2,4,64,1536]{3,2,1,0:T(8,128)(2,1)S(1)}, f32[4,64,1536]{2,1,0:T(8,128)S(1)}, bf16[4,64,1536]{2,1,0:T(8,128)(2,1)S(1)}) custom-call(s32[5]{0:T(128)S(1)} %stack.38.place, bf16[128,1536]{1,0:T(8,128)(2,1)S(1)} %constant_dynamic-update-slice_fusion.b0, bf16[128,1536]{1,0:T(8,128)(2,1)S(1)} %collective-permute-done.7.b1, ...), custom_call_target="tpu_custom_call" | custom-call | flops 2415919104 | bytes 8650752 | tf_op jit(solution)/shard_map/project/pallas_call | solution.py:39
  56.4 2.7 %collective-permute-start.12 = (bf16[64,1536]{1,0:T(8,128)(2,1)S(1)}, bf16[64,1536]{1,0:T(8,128)(2,1)S(1)}, u32[]{:S(2)}, u32[]{:S(2)}) collective-permute-start(bf16[64,1536]{1,0:T(8,128)(2,1)S(1)} %get-tuple-element.33), channel_id=1, source_target_pairs={{0,16},{4,20},{8,24},{12,28},{16,0},{20,4},{24,8},{28,12},{1,17},{... | collective-permute-start | bytes 589832 | tf_op jit(solution)/shard_map/reduce_x/ppermute | solution.py:32
  60.6 2.5 %collective-permute-done.11.p1 = bf16[64,1536]{1,0:T(8,128)(2,1)S(1)} collective-permute-done((bf16[64,1536]{1,0:T(8,128)(2,1)S(1)}, bf16[64,1536]{1,0:T(8,128)(2,1)S(1)}, u32[]{:S(2)}, u32[]{:S(2)}) %collective-permute-start.11) | collective-permute-done | bytes 196640 | tf_op jit(solution)/shard_map/reduce_x/ppermute | solution.py:32
  63.1 5.2 %collective-permute-done.12.p2 = bf16[64,1536]{1,0:T(8,128)(2,1)S(1)} collective-permute-done((bf16[64,1536]{1,0:T(8,128)(2,1)S(1)}, bf16[64,1536]{1,0:T(8,128)(2,1)S(1)}, u32[]{:S(2)}, u32[]{:S(2)}) %collective-permute-start.12) | collective-permute-done | bytes 196640 | tf_op jit(solution)/shard_map/reduce_x/ppermute | solution.py:32
  70.7 2.4 %collective-permute-start.15 = (bf16[64,1536]{1,0:T(8,128)(2,1)S(1)}, bf16[64,1536]{1,0:T(8,128)(2,1)S(1)}, u32[]{:S(2)}, u32[]{:S(2)}) collective-permute-start(bf16[64,1536]{1,0:T(8,128)(2,1)S(1)} %get-tuple-element.35), channel_id=1, source_target_pairs={{0,16},{4,20},{8,24},{12,28},{16,0},{20,4},{24,8},{28,12},{1,17},{... | collective-permute-start | bytes 589832 | tf_op jit(solution)/shard_map/gather_x/ppermute | solution.py:32
  76.7 5.4 %collective-permute-done.15 = bf16[64,1536]{1,0:T(8,128)(2,1)S(1)} collective-permute-done((bf16[64,1536]{1,0:T(8,128)(2,1)S(1)}, bf16[64,1536]{1,0:T(8,128)(2,1)S(1)}, u32[]{:S(2)}, u32[]{:S(2)}) %collective-permute-start.15) | collective-permute-done | bytes 196640 | tf_op jit(solution)/shard_map/gather_x/ppermute | solution.py:32
  82.3 2.3 %collective-permute-done.17.refs_2_.other = bf16[4,64,1536]{2,1,0:T(8,128)(2,1)S(1)} collective-permute-done((bf16[4,64,1536]{2,1,0:T(8,128)(2,1)S(1)}, bf16[4,64,1536]{2,1,0:T(8,128)(2,1)S(1)}, u32[]{:S(2)}, u32[]{:S(2)}) %collective-permute-start.17) | collective-permute-done | bytes 786464 | tf_op jit(solution)/shard_map/gather_x/ppermute | solution.py:32
  84.6 5.1 %back.1 = (f32[128,1536]{1,0:T(8,128)S(1)}, bf16[128,1536]{1,0:T(8,128)(2,1)S(1)}, bf16[128,1536]{1,0:T(8,128)(2,1)S(1)}, bf16[128,1536]{1,0:T(8,128)(2,1)S(1)}) custom-call(s32[5]{0:T(128)S(1)} %stack.38.place, bf16[4,64,1536]{2,1,0:T(8,128)(2,1)S(1)} %pad_maximum_fusion.refs_1_.mine, bf16[4,64,1536]{2,1,0:T(8,128)(2,1)S(1)} %collective-permute-done.17.refs_2_.other, ...), custom_call_target="tpu_custom_call" | custom-call | flops 2415919104 | bytes 7864320 | tf_op jit(solution)/shard_map/back/pallas_call | solution.py:39
  91.0 2.4 %collective-permute-start.19 = (bf16[128,1536]{1,0:T(8,128)(2,1)S(1)}, bf16[128,1536]{1,0:T(8,128)(2,1)S(1)}, u32[]{:S(2)}, u32[]{:S(2)}) collective-permute-start(bf16[128,1536]{1,0:T(8,128)(2,1)S(1)} %get-tuple-element.42), channel_id=1, source_target_pairs={{0,128},{32,160},{1,129},{33,161},{2,130},{34,162},{3,131},{35,163... | collective-permute-start | bytes 1179656 | tf_op jit(solution)/shard_map/reduce_y/ppermute | solution.py:27
  94.9 7.6 %collective-permute-done.18.p1 = bf16[128,1536]{1,0:T(8,128)(2,1)S(1)} collective-permute-done((bf16[128,1536]{1,0:T(8,128)(2,1)S(1)}, bf16[128,1536]{1,0:T(8,128)(2,1)S(1)}, u32[]{:S(2)}, u32[]{:S(2)}) %collective-permute-start.18) | collective-permute-done | bytes 393248 | tf_op jit(solution)/shard_map/reduce_y/ppermute | solution.py:27
  102.5 8.4 %collective-permute-done.19.p2 = bf16[128,1536]{1,0:T(8,128)(2,1)S(1)} collective-permute-done((bf16[128,1536]{1,0:T(8,128)(2,1)S(1)}, bf16[128,1536]{1,0:T(8,128)(2,1)S(1)}, u32[]{:S(2)}, u32[]{:S(2)}) %collective-permute-start.19) | collective-permute-done | bytes 393248 | tf_op jit(solution)/shard_map/reduce_y/ppermute | solution.py:27
  113.3 2.8 %collective-permute-start.22 = (bf16[16,1536]{1,0:T(8,128)(2,1)S(1)}, bf16[16,1536]{1,0:T(8,128)(2,1)S(1)}, u32[]{:S(2)}, u32[]{:S(2)}) collective-permute-start(bf16[16,1536]{1,0:T(8,128)(2,1)S(1)} %get-tuple-element.46), channel_id=1, source_target_pairs={{0,1},{32,33},{1,2},{33,34},{2,3},{34,35},{3,0},{35,32},{64,65},{9... | collective-permute-start | bytes 147464 | tf_op jit(solution)/shard_map/reduce_z/ppermute | solution.py:27
  116.8 4.3 %collective-permute-start.24 = (bf16[16,1536]{1,0:T(8,128)(2,1)S(1)}, bf16[16,1536]{1,0:T(8,128)(2,1)S(1)}, u32[]{:S(2)}, u32[]{:S(2)}) collective-permute-start(bf16[16,1536]{1,0:T(8,128)(2,1)S(1)} %get-tuple-element.48), channel_id=1, source_target_pairs={{0,2},{32,34},{1,3},{33,35},{2,0},{34,32},{3,1},{35,33},{64,66},{9... | collective-permute-start | bytes 147464 | tf_op jit(solution)/shard_map/reduce_z/ppermute | solution.py:27
  122.3 2.3 %collective-permute-start.26 = (bf16[16,1536]{1,0:T(8,128)(2,1)S(1)}, bf16[16,1536]{1,0:T(8,128)(2,1)S(1)}, u32[]{:S(2)}, u32[]{:S(2)}) collective-permute-start(bf16[16,1536]{1,0:T(8,128)(2,1)S(1)} %get-tuple-element.50), channel_id=1, source_target_pairs={{0,3},{32,35},{1,0},{33,32},{2,1},{34,33},{3,2},{35,34},{64,67},{9... | collective-permute-start | bytes 147464 | tf_op jit(solution)/shard_map/reduce_z/ppermute | solution.py:27
  126.2 6.0 %weigh.1 = (bf16[1536,1536]{1,0:T(8,128)(2,1)}, f32[1,1536]{1,0:T(1,128)S(1)}, bf16[4,16,1536]{2,1,0:T(8,128)(2,1)}) custom-call(s32[5]{0:T(128)S(1)} %stack.38.place, bf16[2,4,64,1536]{3,2,1,0:T(8,128)(2,1)S(1)} %get-tuple-element.28.refs_0_, bf16[4,64,1536]{2,1,0:T(8,128)(2,1)S(1)} %pad_maximum_fusion.refs_1_.mine, ...), custom_call_target="tpu_custom_call" | custom-call | flops 2415919104 | bytes 7864320 | tf_op jit(solution)/shard_map/weigh/pallas_call | solution.py:39
  (55 shorter events, 30.2 us)
Async XLA Ops:
  0.6 26.3 %collective-permute-start.5 = (bf16[16,1536]{1,0:T(8,128)(2,1)}, bf16[16,1536]{1,0:T(8,128)(2,1)S(1)}, u32[]{:S(2)}, u32[]{:S(2)}) collective-permute-start(bf16[16,1536]{1,0:T(8,128)(2,1)} %param.4), channel_id=1, source_target_pairs={{0,33},{32,2},{1,34},{33,3},{2,35},{34,0},{3,32},{35,1},{64,97},{9... | collective-permute-start | bytes 147464 | tf_op jit(solution)/shard_map/gather_z/ppermute | solution.py:27
  6.5 20.4 %collective-permute-start.4 = (bf16[16,1536]{1,0:T(8,128)(2,1)}, bf16[16,1536]{1,0:T(8,128)(2,1)S(1)}, u32[]{:S(2)}, u32[]{:S(2)}) collective-permute-start(bf16[16,1536]{1,0:T(8,128)(2,1)} %param.4), channel_id=1, source_target_pairs={{0,34},{32,3},{1,35},{33,0},{2,32},{34,1},{3,33},{35,2},{64,98},{9... | collective-permute-start | bytes 147464 | tf_op jit(solution)/shard_map/gather_z/ppermute | solution.py:27
  6.6 20.2 %collective-permute-start.3 = (bf16[16,1536]{1,0:T(8,128)(2,1)}, bf16[16,1536]{1,0:T(8,128)(2,1)S(1)}, u32[]{:S(2)}, u32[]{:S(2)}) collective-permute-start(bf16[16,1536]{1,0:T(8,128)(2,1)} %param.4), channel_id=1, source_target_pairs={{0,35},{32,0},{1,32},{33,1},{2,33},{34,2},{3,34},{35,3},{64,99},{9... | collective-permute-start | bytes 147464 | tf_op jit(solution)/shard_map/gather_z/ppermute | solution.py:27
  7.7 19.2 %collective-permute-start.2 = (bf16[16,1536]{1,0:T(8,128)(2,1)}, bf16[16,1536]{1,0:T(8,128)(2,1)S(1)}, u32[]{:S(2)}, u32[]{:S(2)}) collective-permute-start(bf16[16,1536]{1,0:T(8,128)(2,1)} %param.4), channel_id=1, source_target_pairs={{0,1},{32,33},{1,2},{33,34},{2,3},{34,35},{3,0},{35,32},{64,65},{9... | collective-permute-start | bytes 147464 | tf_op jit(solution)/shard_map/gather_z/ppermute | solution.py:27
  16.2 8.7 %collective-permute-start.1 = (bf16[16,1536]{1,0:T(8,128)(2,1)}, bf16[16,1536]{1,0:T(8,128)(2,1)S(1)}, u32[]{:S(2)}, u32[]{:S(2)}) collective-permute-start(bf16[16,1536]{1,0:T(8,128)(2,1)} %param.4), channel_id=1, source_target_pairs={{0,2},{32,34},{1,3},{33,35},{2,0},{34,32},{3,1},{35,33},{64,66},{9... | collective-permute-start | bytes 147464 | tf_op jit(solution)/shard_map/gather_z/ppermute | solution.py:27
  29.3 13.2 %collective-permute-start.9 = (bf16[128,1536]{1,0:T(8,128)(2,1)S(1)}, bf16[128,1536]{1,0:T(8,128)(2,1)S(1)}, u32[]{:S(2)}, u32[]{:S(2)}) collective-permute-start(bf16[128,1536]{1,0:T(8,128)(2,1)S(1)} %constant_dynamic-update-slice_fusion.b0), channel_id=1, source_target_pairs={{0,64},{32,96},{1,65},{33,97},{2,66},{34,98},{3,67},{35,99},{64,12... | collective-permute-start | bytes 1179656 | tf_op jit(solution)/shard_map/gather_y/ppermute | solution.py:27
  30.9 16.4 %collective-permute-start.8 = (bf16[128,1536]{1,0:T(8,128)(2,1)S(1)}, bf16[128,1536]{1,0:T(8,128)(2,1)S(1)}, u32[]{:S(2)}, u32[]{:S(2)}) collective-permute-start(bf16[128,1536]{1,0:T(8,128)(2,1)S(1)} %constant_dynamic-update-slice_fusion.b0), channel_id=1, source_target_pairs={{0,128},{32,160},{1,129},{33,161},{2,130},{34,162},{3,131},{35,163... | collective-permute-start | bytes 1179656 | tf_op jit(solution)/shard_map/gather_y/ppermute | solution.py:27
  33.8 13.5 %collective-permute-start.7 = (bf16[128,1536]{1,0:T(8,128)(2,1)S(1)}, bf16[128,1536]{1,0:T(8,128)(2,1)S(1)}, u32[]{:S(2)}, u32[]{:S(2)}) collective-permute-start(bf16[128,1536]{1,0:T(8,128)(2,1)S(1)} %constant_dynamic-update-slice_fusion.b0), channel_id=1, source_target_pairs={{0,192},{32,224},{1,193},{33,225},{2,194},{34,226},{3,195},{35,227... | collective-permute-start | bytes 1179656 | tf_op jit(solution)/shard_map/gather_y/ppermute | solution.py:27
  54.9 8.2 %collective-permute-start.11 = (bf16[64,1536]{1,0:T(8,128)(2,1)S(1)}, bf16[64,1536]{1,0:T(8,128)(2,1)S(1)}, u32[]{:S(2)}, u32[]{:S(2)}) collective-permute-start(bf16[64,1536]{1,0:T(8,128)(2,1)S(1)} %get-tuple-element.32), channel_id=1, source_target_pairs={{0,8},{4,12},{8,16},{12,20},{16,24},{20,28},{24,0},{28,4},{1,9},{5... | collective-permute-start | bytes 589832 | tf_op jit(solution)/shard_map/reduce_x/ppermute | solution.py:32
  56.4 11.9 %collective-permute-start.12 = (bf16[64,1536]{1,0:T(8,128)(2,1)S(1)}, bf16[64,1536]{1,0:T(8,128)(2,1)S(1)}, u32[]{:S(2)}, u32[]{:S(2)}) collective-permute-start(bf16[64,1536]{1,0:T(8,128)(2,1)S(1)} %get-tuple-element.33), channel_id=1, source_target_pairs={{0,16},{4,20},{8,24},{12,28},{16,0},{20,4},{24,8},{28,12},{1,17},{... | collective-permute-start | bytes 589832 | tf_op jit(solution)/shard_map/reduce_x/ppermute | solution.py:32
  59.2 9.1 %collective-permute-start.13 = (bf16[64,1536]{1,0:T(8,128)(2,1)S(1)}, bf16[64,1536]{1,0:T(8,128)(2,1)S(1)}, u32[]{:S(2)}, u32[]{:S(2)}) collective-permute-start(bf16[64,1536]{1,0:T(8,128)(2,1)S(1)} %get-tuple-element.34), channel_id=1, source_target_pairs={{0,24},{4,28},{8,0},{12,4},{16,8},{20,12},{24,16},{28,20},{1,25},{... | collective-permute-start | bytes 589832 | tf_op jit(solution)/shard_map/reduce_x/ppermute | solution.py:32
  69.3 7.4 %collective-permute-start.16 = (bf16[64,1536]{1,0:T(8,128)(2,1)S(1)}, bf16[64,1536]{1,0:T(8,128)(2,1)S(1)}, u32[]{:S(2)}, u32[]{:S(2)}) collective-permute-start(bf16[64,1536]{1,0:T(8,128)(2,1)S(1)} %get-tuple-element.35), channel_id=1, source_target_pairs={{0,8},{4,12},{8,16},{12,20},{16,24},{20,28},{24,0},{28,4},{1,9},{5... | collective-permute-start | bytes 589832 | tf_op jit(solution)/shard_map/gather_x/ppermute | solution.py:32
  70.7 11.4 %collective-permute-start.15 = (bf16[64,1536]{1,0:T(8,128)(2,1)S(1)}, bf16[64,1536]{1,0:T(8,128)(2,1)S(1)}, u32[]{:S(2)}, u32[]{:S(2)}) collective-permute-start(bf16[64,1536]{1,0:T(8,128)(2,1)S(1)} %get-tuple-element.35), channel_id=1, source_target_pairs={{0,16},{4,20},{8,24},{12,28},{16,0},{20,4},{24,8},{28,12},{1,17},{... | collective-permute-start | bytes 589832 | tf_op jit(solution)/shard_map/gather_x/ppermute | solution.py:32
  73.1 9.0 %collective-permute-start.14 = (bf16[64,1536]{1,0:T(8,128)(2,1)S(1)}, bf16[64,1536]{1,0:T(8,128)(2,1)S(1)}, u32[]{:S(2)}, u32[]{:S(2)}) collective-permute-start(bf16[64,1536]{1,0:T(8,128)(2,1)S(1)} %get-tuple-element.35), channel_id=1, source_target_pairs={{0,24},{4,28},{8,0},{12,4},{16,8},{20,12},{24,16},{28,20},{1,25},{... | collective-permute-start | bytes 589832 | tf_op jit(solution)/shard_map/gather_x/ppermute | solution.py:32
  89.6 12.9 %collective-permute-start.18 = (bf16[128,1536]{1,0:T(8,128)(2,1)S(1)}, bf16[128,1536]{1,0:T(8,128)(2,1)S(1)}, u32[]{:S(2)}, u32[]{:S(2)}) collective-permute-start(bf16[128,1536]{1,0:T(8,128)(2,1)S(1)} %get-tuple-element.41), channel_id=1, source_target_pairs={{0,64},{32,96},{1,65},{33,97},{2,66},{34,98},{3,67},{35,99},{64,12... | collective-permute-start | bytes 1179656 | tf_op jit(solution)/shard_map/reduce_y/ppermute | solution.py:27
  91.0 19.9 %collective-permute-start.19 = (bf16[128,1536]{1,0:T(8,128)(2,1)S(1)}, bf16[128,1536]{1,0:T(8,128)(2,1)S(1)}, u32[]{:S(2)}, u32[]{:S(2)}) collective-permute-start(bf16[128,1536]{1,0:T(8,128)(2,1)S(1)} %get-tuple-element.42), channel_id=1, source_target_pairs={{0,128},{32,160},{1,129},{33,161},{2,130},{34,162},{3,131},{35,163... | collective-permute-start | bytes 1179656 | tf_op jit(solution)/shard_map/reduce_y/ppermute | solution.py:27
  93.3 17.8 %collective-permute-start.20 = (bf16[128,1536]{1,0:T(8,128)(2,1)S(1)}, bf16[128,1536]{1,0:T(8,128)(2,1)S(1)}, u32[]{:S(2)}, u32[]{:S(2)}) collective-permute-start(bf16[128,1536]{1,0:T(8,128)(2,1)S(1)} %get-tuple-element.43), channel_id=1, source_target_pairs={{0,192},{32,224},{1,193},{33,225},{2,194},{34,226},{3,195},{35,227... | collective-permute-start | bytes 1179656 | tf_op jit(solution)/shard_map/reduce_y/ppermute | solution.py:27
  111.3 11.0 %collective-permute-start.21 = (bf16[16,1536]{1,0:T(8,128)(2,1)S(1)}, bf16[16,1536]{1,0:T(8,128)(2,1)S(1)}, u32[]{:S(2)}, u32[]{:S(2)}) collective-permute-start(bf16[16,1536]{1,0:T(8,128)(2,1)S(1)} %get-tuple-element.45), channel_id=1, source_target_pairs={{0,32},{32,1},{1,33},{33,2},{2,34},{34,3},{3,35},{35,0},{64,96},{9... | collective-permute-start | bytes 147464 | tf_op jit(solution)/shard_map/reduce_z/ppermute | solution.py:27
  113.3 11.4 %collective-permute-start.22 = (bf16[16,1536]{1,0:T(8,128)(2,1)S(1)}, bf16[16,1536]{1,0:T(8,128)(2,1)S(1)}, u32[]{:S(2)}, u32[]{:S(2)}) collective-permute-start(bf16[16,1536]{1,0:T(8,128)(2,1)S(1)} %get-tuple-element.46), channel_id=1, source_target_pairs={{0,1},{32,33},{1,2},{33,34},{2,3},{34,35},{3,0},{35,32},{64,65},{9... | collective-permute-start | bytes 147464 | tf_op jit(solution)/shard_map/reduce_z/ppermute | solution.py:27
  116.1 16.8 %collective-permute-start.23 = (bf16[16,1536]{1,0:T(8,128)(2,1)S(1)}, bf16[16,1536]{1,0:T(8,128)(2,1)S(1)}, u32[]{:S(2)}, u32[]{:S(2)}) collective-permute-start(bf16[16,1536]{1,0:T(8,128)(2,1)S(1)} %get-tuple-element.47), channel_id=1, source_target_pairs={{0,33},{32,2},{1,34},{33,3},{2,35},{34,0},{3,32},{35,1},{64,97},{9... | collective-permute-start | bytes 147464 | tf_op jit(solution)/shard_map/reduce_z/ppermute | solution.py:27
  116.8 16.0 %collective-permute-start.24 = (bf16[16,1536]{1,0:T(8,128)(2,1)S(1)}, bf16[16,1536]{1,0:T(8,128)(2,1)S(1)}, u32[]{:S(2)}, u32[]{:S(2)}) collective-permute-start(bf16[16,1536]{1,0:T(8,128)(2,1)S(1)} %get-tuple-element.48), channel_id=1, source_target_pairs={{0,2},{32,34},{1,3},{33,35},{2,0},{34,32},{3,1},{35,33},{64,66},{9... | collective-permute-start | bytes 147464 | tf_op jit(solution)/shard_map/reduce_z/ppermute | solution.py:27
  121.1 11.7 %collective-permute-start.25 = (bf16[16,1536]{1,0:T(8,128)(2,1)S(1)}, bf16[16,1536]{1,0:T(8,128)(2,1)S(1)}, u32[]{:S(2)}, u32[]{:S(2)}) collective-permute-start(bf16[16,1536]{1,0:T(8,128)(2,1)S(1)} %get-tuple-element.49), channel_id=1, source_target_pairs={{0,34},{32,3},{1,35},{33,0},{2,32},{34,1},{3,33},{35,2},{64,98},{9... | collective-permute-start | bytes 147464 | tf_op jit(solution)/shard_map/reduce_z/ppermute | solution.py:27
  122.3 10.5 %collective-permute-start.26 = (bf16[16,1536]{1,0:T(8,128)(2,1)S(1)}, bf16[16,1536]{1,0:T(8,128)(2,1)S(1)}, u32[]{:S(2)}, u32[]{:S(2)}) collective-permute-start(bf16[16,1536]{1,0:T(8,128)(2,1)S(1)} %get-tuple-element.50), channel_id=1, source_target_pairs={{0,3},{32,35},{1,0},{33,32},{2,1},{34,33},{3,2},{35,34},{64,67},{9... | collective-permute-start | bytes 147464 | tf_op jit(solution)/shard_map/reduce_z/ppermute | solution.py:27
  124.7 8.2 %collective-permute-start.27 = (bf16[16,1536]{1,0:T(8,128)(2,1)S(1)}, bf16[16,1536]{1,0:T(8,128)(2,1)S(1)}, u32[]{:S(2)}, u32[]{:S(2)}) collective-permute-start(bf16[16,1536]{1,0:T(8,128)(2,1)S(1)} %get-tuple-element.51), channel_id=1, source_target_pairs={{0,35},{32,0},{1,32},{33,1},{2,33},{34,2},{3,34},{35,3},{64,99},{9... | collective-permute-start | bytes 147464 | tf_op jit(solution)/shard_map/reduce_z/ppermute | solution.py:27
  (6 other events, 74.7 us)

commit v2 on v0

v2 whole, which is shorter than its diff:
```python
import math

import jax
import jax.numpy as jnp
from jax import lax
from jax.experimental import pallas as pl
from jax.experimental.pallas import tpu as pltpu
from jax.sharding import PartitionSpec as P

CHUNKS = ((0, 2), (1, 3))
BF = jnp.bfloat16
F32 = jnp.float32
ROW = 16
LIMIT = 24 * 1024 * 1024
PLANE = ("gx", "gz")
FAST = pl.BlockSpec(memory_space=pltpu.VMEM)
SMEM = pl.BlockSpec(memory_space=pltpu.SMEM)
ANY = pl.BlockSpec(memory_space=pl.ANY)


def by_plane(array, dy, dh, flip=0):
    flat = lambda y, h, l: (y % 4 * 2 + l) * 4 + h % 4
    pairs = [
        (flat(y, h, l), flat(y + dy, h + dh, l ^ flip)) for y in range(4) for h in range(4) for l in range(2)
    ]
    return lax.ppermute(array, PLANE, pairs)


def by_line(array, dx, flip=0):
    pairs = [(2 * x + c, (x + dx) % 4 * 2 + (c ^ flip)) for x in range(4) for c in range(2)]
    return lax.ppermute(array, "gy", pairs)


def call(body, ins, outs, scratch=(), flops=0, moved=0, place=None, grid=(), out_specs=None, after=(), sources=()):
    in_specs = [FAST] * len(ins)
    if place is not None:
        ins, in_specs = [place, *ins], [SMEM, *in_specs]
    ins, in_specs = [*ins, *sources], [*in_specs, *[ANY] * len(sources)]
    used = len(ins)
    ins, in_specs = [*ins, *after], [*in_specs, *[ANY] * len(after)]

    def run(*refs):
        body(*refs[:used], *refs[used + len(after) :])

    return pl.pallas_call(
        run,
        grid=grid,
        in_specs=in_specs,
        out_specs=out_specs or [FAST] * len(outs),
        out_shape=[o if isinstance(o, pl.MemoryRef) else jax.ShapeDtypeStruct(*o) for o in outs],
        scratch_shapes=list(scratch),
        compiler_params=pltpu.CompilerParams(vmem_limit_bytes=LIMIT),
        cost_estimate=pl.CostEstimate(flops=flops, bytes_accessed=moved, transcendentals=0),
    )(*ins)


def fetch(arrays, after):
    def body(*refs):
        ins, outs, done = refs[: len(arrays)], refs[len(arrays) : -1], refs[-1]
        copies = [pltpu.make_async_copy(a, b, done.at[i]) for i, (a, b) in enumerate(zip(ins, outs))]
        for copy in copies:
            copy.start()
        for copy in copies:
            copy.wait()

    return call(
        body,
        [],
        [pltpu.VMEM(a.shape, a.dtype) for a in arrays],
        scratch=[pltpu.SemaphoreType.DMA((len(arrays),))],
        moved=sum(2 * a.size * a.dtype.itemsize for a in arrays),
        sources=[pltpu.with_memory_space_constraint(a, pltpu.HBM) for a in arrays],
        after=after,
    )


def bundle(parts, after=()):
    count = sum(math.prod(p.shape[:-2]) for p in parts)
    width = parts[0].shape[-1]

    def body(*refs):
        at = 0
        for ref in refs[:-1]:
            size = math.prod(ref.shape[:-2])
            refs[-1][at : at + size] = ref[...].reshape(size, ROW, width)
            at += size

    return call(
        body, list(parts), [((count, ROW, width), BF)], moved=4 * count * ROW * width, after=after
    )[0]


def project(place, blocks, w_in, tile=512):
    count = blocks[0].shape[0]
    depth, width = w_in.shape
    rows = 8 * count * ROW

    def body(place, b0, b1, b2, b3, w, held, keep, give):
        x, c, y, l = (place[i] for i in range(4))
        for t, block in enumerate((b0, b1, b2, b3)):
            at = (y + t - x + 4) % 4
            for p in range(2):
                side = (l + p + c) % 2
                for e in range(count):
                    held[side, at, e] = block[e, p]
        for j in range(width // tile):
            cut = slice(j * tile, (j + 1) * tile)
            found = jnp.dot(held[...].reshape(rows, depth), w[:, cut], preferred_element_type=F32)
            keep[:, :, cut] = found[: rows // 2].reshape(4, count * ROW, tile)
            give[:, :, cut] = found[rows // 2 :].reshape(4, count * ROW, tile).astype(BF)

    return call(
        body,
        [*blocks, w_in],
        [
            ((2, 4, count, ROW, depth), BF),
            ((4, count * ROW, width), F32),
            ((4, count * ROW, width), BF),
        ],
        flops=2 * rows * depth * width,
        moved=2 * depth * width + 5 * rows * width,
        place=place,
    )


def add_pair(keep, got):
    _, half, width = keep.shape

    def body(keep, got, own, *rest):
        own[...] = keep[0] + got[0].astype(F32)
        for d, out in enumerate(rest, 1):
            out[...] = (keep[d] + got[d].astype(F32)).astype(BF)

    return call(
        body,
        [keep, got],
        [((half, width), F32)] + [((half, width), BF)] * 3,
        flops=keep.size,
        moved=8 * keep.size,
    )


def bend(place, own, parts, bias, grad_act, chunk):
    half, width = own.shape
    coef = math.sqrt(2.0 / math.pi)

    def body(place, own, p1, p2, p3, bias, grad_act, act, grad):
        for j, e in enumerate(chunk):
            here = slice(j * ROW, (j + 1) * ROW)
            at = (place[4] + e) % 4
            v = own[here, :] + p1[here, :].astype(F32)
            v = v + (p2[here, :].astype(F32) + p3[here, :].astype(F32)) + bias[...]
            t = jnp.tanh(coef * (v + 0.044715 * v * v * v))
            act[here, :] = (0.5 * v * (1.0 + t)).astype(BF)
            slope = 0.5 * (1.0 + t) + 0.5 * v * (1.0 - t * t) * coef * (1.0 + 3.0 * 0.044715 * v * v)
            grad[here, :] = (grad_act[at].astype(F32) * slope).astype(BF)

    return call(
        body,
        [own, *parts, bias, grad_act],
        [((half, width), BF)] * 2,
        flops=30 * own.size,
        moved=14 * own.size,
        place=place,
    )


def back(place, mine, other, w_in, tile=512):
    _, half, width = mine.shape
    count = half // ROW
    depth = w_in.shape[0]
    rows = 8 * half

    def body(place, mine, other, w, o0, o1, o2, o3, all_rows, found):
        x, c, y, l = (place[i] for i in range(4))
        all_rows[: rows // 2] = mine[...].reshape(rows // 2, width)
        all_rows[rows // 2 :] = other[...].reshape(rows // 2, width)
        turn = (((1,), (1,)), ((), ()))
        for j in range(depth // tile):
            cut = slice(j * tile, (j + 1) * tile)
            product = lax.dot_general(all_rows[...], w[cut, :], turn, preferred_element_type=F32)
            found[...] = product.reshape(2, 4, count, ROW, tile)
            for t, out in enumerate((o0, o1, o2, o3)):
                at = (y + t - x + 4) % 4
                for p in range(2):
                    side = (l + p + c) % 2
                    for e in range(count):
                        out[e, p, :, cut] = found[side, at, e].astype(out.dtype)

    return call(
        body,
        [mine, other, w_in],
        [((count, 2, ROW, depth), F32 if t == 0 else BF) for t in range(4)],
        scratch=[pltpu.VMEM((rows, width), BF), pltpu.VMEM((2, 4, count, ROW, tile), F32)],
        flops=2 * rows * depth * width,
        moved=2 * depth * width + 4 * rows * width,
        place=place,
    )


def add_four(own, parts, chunk, after):
    _, _, _, width = own.shape

    def body(own, p1, p2, p3, *outs):
        for j, out in enumerate(outs):
            v = own[j] + p1[j].astype(F32)
            v = v + (p2[j].astype(F32) + p3[j].astype(F32))
            out[...] = v.astype(out.dtype)

    return call(
        body,
        [own, *parts],
        [((2, ROW, width), BF if e else F32) for e in chunk],
        flops=3 * own.size,
        moved=12 * own.size,
        after=after,
    )


def add_rest(arrays):
    width = arrays[0].shape[2]

    def body(*refs):
        total = refs[0][...].astype(F32)
        for ref in refs[1:-2]:
            total = total + ref[...].astype(F32)
        refs[-2][...] = total[0]
        refs[-1][...] = total[1].astype(BF)

    return call(
        body,
        list(arrays),
        [((ROW, width), F32), ((ROW, width), BF)],
        flops=8 * ROW * width,
        moved=18 * ROW * width,
    )


def add_last(own, got):
    def body(own, got, out):
        out[...] = (own[...] + got[...].astype(F32)).astype(BF)

    return call(body, [own, got], [(own.shape, BF)], flops=own.size, moved=8 * own.size)[0]


def settle(place, grads, acts, after):
    width = grads[0].shape[2]

    def body(place, *refs):
        total = jnp.zeros((1, width), F32)
        for ref in refs[: len(grads)]:
            part = ref[...].reshape(-1, width).astype(F32)
            total = total + jnp.sum(part, axis=0, keepdims=True)
        bias, act = refs[-2:]
        bias[...] = total
        for chunk, ref in zip(CHUNKS, refs[len(grads) : -2]):
            for j, e in enumerate(chunk):
                act[(place[4] + e) % 4] = ref[j * ROW : (j + 1) * ROW, :]

    return call(
        body,
        [*grads, *acts],
        [((1, width), F32), ((4, ROW, width), BF)],
        flops=512 * width,
        moved=1024 * width,
        place=place,
        after=after,
    )


def weigh(held, grads, after, tile=512):
    depth = held[0].shape[-1]
    width = grads[0].shape[-1]
    rows = 32 * ROW

    def body(*refs):
        sources, (weight, done, left, right) = refs[:-4], refs[-4:]

        @pl.when(pl.program_id(0) == 0)
        def _():
            done[...] = jnp.zeros_like(done)
            for into, parts in ((left, sources[: len(held)]), (right, sources[len(held) :])):
                at = 0
                for part in parts:
                    size = math.prod(part.shape[:-1])
                    into[at : at + size] = part[...].reshape(size, part.shape[-1])
                    at += size

        cut = pl.ds(pl.multiple_of(pl.program_id(0) * tile, tile), tile)
        weight[...] = lax.dot_general(
            left[:, cut], right[...], (((0,), (0,)), ((), ())), preferred_element_type=F32
        ).astype(BF)

    return call(
        body,
        [*held, *grads],
        [((depth, width), BF), ((8, 128), F32)],
        scratch=[pltpu.VMEM((rows, depth), BF), pltpu.VMEM((rows, width), BF)],
        flops=2 * rows * depth * width,
        moved=2 * depth * width + 4 * rows * width,
        grid=(depth // tile,),
        out_specs=[pl.BlockSpec((tile, width), lambda j: (j, 0)), pl.BlockSpec((8, 128), lambda j: (0, 0))],
        after=after,
    )


def on_device(tokens, w_in, bias, grad_act):
    gx, gy, gz = (lax.axis_index(a) for a in ("gx", "gy", "gz"))
    place = jnp.stack([gy // 2, gy % 2, gx // 2, gx % 2, gz]).astype(jnp.int32)
    width = w_in.shape[1]
    bias = bias.reshape(1, width)
    grad_act = grad_act.reshape(4, ROW, width)

    with jax.named_scope("gather_z"):
        flipped = by_plane(tokens, 0, 0, 1)
        far = [by_plane(tokens, 0, -2), by_plane(tokens, 0, -2, 1)]
        w_in, local = fetch([w_in, tokens], [place])
        first = bundle([local, flipped, *far])
        pair = first[:2]
    blocks = []
    for k, chunk in enumerate(CHUNKS):
        with jax.named_scope("gather_z"):
            if k:
                first = bundle([by_plane(pair, 0, -e) for e in chunk], after=[blocks[0][1], blocks[0][3]])
            own = first.reshape(2, 2, ROW, tokens.shape[1])
        with jax.named_scope("gather_y"):
            blocks.append([own] + [by_plane(own, -t, 0) for t in (1, 2, 3)])
    held, acts, grads, ends = [], [], [], {}
    for chunk, block in zip(CHUNKS, blocks):
        with jax.named_scope("project"):
            order, keep, give = project(place, block, w_in)
            held.append(order)
        with jax.named_scope("reduce_x"):
            own, *parts = add_pair(keep, by_line(give, 0, 1))
            parts = [by_line(p, d) for d, p in enumerate(parts, 1)]
        with jax.named_scope("bend"):
            act, grad = bend(place, own, parts, bias, grad_act, chunk)
            acts.append(act)
        with jax.named_scope("gather_x"):
            mine = jnp.stack([grad] + [by_line(grad, -d) for d in (1, 2, 3)])
            grads += [mine, by_line(mine, 0, 1)]
    partials = []
    for k, chunk in enumerate(CHUNKS):
        with jax.named_scope("back"):
            own, *parts = back(place, *grads[2 * k : 2 * k + 2], w_in)
        with jax.named_scope("reduce_y"):
            partials.append([own] + [by_plane(p, t, 0) for t, p in enumerate(parts, 1)])
    with jax.named_scope("settle"):
        grad_bias, act = settle(place, grads, acts, [partials[1][0]])
    with jax.named_scope("weigh"):
        grad_weight, weighed = weigh(held, grads, [partials[1][0]])
    for (own, *parts), chunk, beside in zip(partials, CHUNKS, (grad_bias, weighed)):
        with jax.named_scope("reduce_y"):
            sums = add_four(own, parts, chunk, [beside])
        with jax.named_scope("reduce_z"):
            for e, part in zip(chunk, sums):
                ends[e] = by_plane(part, 0, e) if e else part
    with jax.named_scope("reduce_z"):
        own, part = add_rest([ends[e] for e in range(4)])
        part = by_plane(part, 0, 0, 1)
    with jax.named_scope("finish"):
        grad_tokens = add_last(own, part)
    return (act.reshape(4 * ROW, width), grad_bias.reshape(width), grad_weight, grad_tokens)


def solution(mesh):
    placed = (P(("gx", "gz"), "gy"), P("gy", ("gx", "gz")), P(("gx", "gz")), P("gy", ("gx", "gz")))
    return jax.shard_map(
        on_device,
        mesh=mesh,
        in_specs=placed,
        out_specs=(
            P("gy", ("gx", "gz")),
            P(("gx", "gz")),
            P("gy", ("gx", "gz")),
            P(("gx", "gz"), "gy"),
        ),
        check_vma=False,
    )
```

time: 402 us -> 105 us (0.26); the launches traced: 397 us -> 105 us
  waiting for transfers between devices: 340 us -> 29.1 us
  starting transfers between devices: 0.16 us -> 55.3 us
  Pallas kernels: 0 us -> 18.9 us
  matrix products: 18.5 us -> 0 us
  blocking collectives: 14.4 us -> 0 us
  between operations: 13.8 us -> 0.85 us
  local copies, waits for them, and re-layouts: 6.64 us -> 0.11 us
    all_gather x2 -> x0, waiting for transfers between devices: 174 us -> none  [the longest x1 148 us: on_device(): gathered = lax.all_gather(tokens, ('gx', 'gz'), axis=0, tiled=True)]
    reduce_scatter x2 -> x0, waiting for transfers between devices: 165 us -> none  [the longest x1 128 us: on_device(): lax.psum_scatter(lax.dot_general(block, w_in, (((1,), (1,)), ((), ())), p...]
    ppermute x0 -> x37, starting transfers between devices: none -> 55.3 us  [the longest x21 36.7 us: by_plane(): return lax.ppermute(array, PLANE, pairs)]
    ppermute x0 -> x37, waiting for transfers between devices: none -> 29.1 us  [the longest x21 24.1 us: by_plane(): return lax.ppermute(array, PLANE, pairs)]
    pallas_call x0 -> x17, Pallas kernels: none -> 18.9 us  [call(): pl.pallas_call(run, grid=grid, in_specs=in_specs, out_specs=out_specs or...]
    dot_general x3 -> x0, matrix products: 18.5 us -> none  [the longest x1 7.1 us: on_device(): lax.dot_general(block, w_in, (((1,), (1,)), ((), ())), preferred_element_...]
    psum x1 -> x0, blocking collectives: 14.4 us -> none  [on_device(): grad_bias = lax.psum(jnp.sum(grad_pre, axis=0, dtype=jnp.float32), 'gy')]
    unnamed x9 -> x4, local copies, waits for them, and re-layouts: 6.64 us -> 0.01 us
  transfers between devices with their start and end apart: 4 -> 37, of which waited for: 4 -> 12; matrix products, arithmetic and copies ran while one was open for 3% -> 1% of each run, Pallas kernels for 0% -> 17%
where the time goes in v2:
time: 105 us
  starting transfers between devices  55.3 us (53%)
  waiting for transfers between devices  29.1 us (28%)
  Pallas kernels  18.9 us (18%)
    ppermute x21, starting transfers between devices, by_plane(): return lax.ppermute(array, PLANE, pairs)  36.7 us
    ppermute x21, waiting for transfers between devices, by_plane(): return lax.ppermute(array, PLANE, pairs)  24.1 us
    pallas_call x17, Pallas kernels, call(): pl.pallas_call(run, grid=grid, in_specs=in_specs, out_specs=out_specs or...  18.9 us
    ppermute x16, starting transfers between devices, by_line(): return lax.ppermute(array, 'gy', pairs)  18.6 us
    ppermute x16, waiting for transfers between devices, by_line(): return lax.ppermute(array, 'gy', pairs)  5.05 us
  transfers between devices with their start and end apart: 37, of which 12 were waited for; matrix products, arithmetic and copies ran while one was open for 1% of the time, Pallas kernels for 17%

profile of v2, /device:TPU:32, one launch (start us, length us, event | category | flops | bytes accessed | tf_op | source)
XLA Modules:
  0.0 105.0 jit_solution(11477085703583649082)
XLA Ops:
  0.6 1.9 %collective-permute-start = (bf16[16,1536]{1,0:T(8,128)(2,1)}, bf16[16,1536]{1,0:T(8,128)(2,1)S(1)}, u32[]{:S(2)}, u32[]{:S(2)}) collective-permute-start(bf16[16,1536]{1,0:T(8,128)(2,1)} %refs_1_.1), channel_id=1, source_target_pairs={{0,32},{32,0},{1,33},{33,1},{2,34},{34,2},{3,35},{35,3},{64,96},{9... | collective-permute-start | bytes 147464 | tf_op jit(solution)/shard_map/gather_z/ppermute | solution.py:26
  2.6 5.0 %collective-permute-start.2 = (bf16[16,1536]{1,0:T(8,128)(2,1)}, bf16[16,1536]{1,0:T(8,128)(2,1)S(1)}, u32[]{:S(2)}, u32[]{:S(2)}) collective-permute-start(bf16[16,1536]{1,0:T(8,128)(2,1)} %refs_1_.1), channel_id=1, source_target_pairs={{0,34},{32,2},{1,35},{33,3},{2,32},{34,0},{3,33},{35,1},{64,98},{9... | collective-permute-start | bytes 147464 | tf_op jit(solution)/shard_map/gather_z/ppermute | solution.py:26
  8.1 2.4 %gather_z.3 = (bf16[1536,1536]{1,0:T(8,128)(2,1)S(1)}, bf16[16,1536]{1,0:T(8,128)(2,1)S(1)}) custom-call(bf16[1536,1536]{1,0:T(8,128)(2,1)} %refs_0_.1, bf16[16,1536]{1,0:T(8,128)(2,1)} %refs_1_.1, s32[5]{0:T(128)S(1)} %stack.53.refs_2_.refs_0_), custom_call_target="tpu_custom_call" | custom-call | bytes 9535488 | tf_op jit(solution)/shard_map/gather_z/pallas_call | solution.py:45
  10.5 6.0 %collective-permute-done.1.refs_2_ = bf16[16,1536]{1,0:T(8,128)(2,1)S(1)} collective-permute-done((bf16[16,1536]{1,0:T(8,128)(2,1)}, bf16[16,1536]{1,0:T(8,128)(2,1)S(1)}, u32[]{:S(2)}, u32[]{:S(2)}) %collective-permute-start.1) | collective-permute-done | bytes 49184 | tf_op jit(solution)/shard_map/gather_z/ppermute | solution.py:26
  19.8 2.0 %collective-permute-start.4 = (bf16[2,2,16,1536]{3,2,1,0:T(8,128)(2,1)S(1)}, bf16[2,2,16,1536]{3,2,1,0:T(8,128)(2,1)S(1)}, u32[]{:S(2)}, u32[]{:S(2)}) collective-permute-start(bf16[2,2,16,1536]{3,2,1,0:T(8,128)(2,1)S(1)} %bitcast.19), channel_id=1, source_target_pairs={{0,128},{32,160},{1,129},{33,161},{2,130},{34,162},{3,131},{35,163... | collective-permute-start | bytes 589832 | tf_op jit(solution)/shard_map/gather_y/ppermute | solution.py:26
  23.2 2.8 %collective-permute-start.14 = (bf16[2,16,1536]{2,1,0:T(8,128)(2,1)S(1)}, bf16[2,16,1536]{2,1,0:T(8,128)(2,1)S(1)}, u32[]{:S(2)}, u32[]{:S(2)}) collective-permute-start(bf16[2,16,1536]{2,1,0:T(8,128)(2,1)S(1)} %slice.4), channel_id=1, source_target_pairs={{0,3},{32,35},{1,0},{33,32},{2,1},{34,33},{3,2},{35,34},{64,67},{9... | collective-permute-start | bytes 294920 | tf_op jit(solution)/shard_map/gather_z/ppermute | solution.py:26
  26.0 3.6 %collective-permute-done.15.refs_1_ = bf16[2,16,1536]{2,1,0:T(8,128)(2,1)S(1)} collective-permute-done((bf16[2,16,1536]{2,1,0:T(8,128)(2,1)S(1)}, bf16[2,16,1536]{2,1,0:T(8,128)(2,1)S(1)}, u32[]{:S(2)}, u32[]{:S(2)}) %collective-permute-start.15) | collective-permute-done | bytes 98336 | tf_op jit(solution)/shard_map/gather_z/ppermute | solution.py:26
  33.9 2.0 %project.2 = (bf16[2,4,2,16,1536]{4,3,2,1,0:T(8,128)(2,1)S(1)}, f32[4,32,1536]{2,1,0:T(8,128)S(1)}, bf16[4,32,1536]{2,1,0:T(8,128)(2,1)S(1)}) custom-call(s32[5]{0:T(128)S(1)} %stack.53.refs_2_.refs_0_, bf16[2,2,16,1536]{3,2,1,0:T(8,128)(2,1)S(1)} %bitcast.20, bf16[2,2,16,1536]{3,2,1,0:T(8,128)(2,1)S(1)} %collective-permute-done.3.refs_2_, ...), custom_call_target="tpu_custom_call" | custom-call | flops 1207959552 | bytes 6684672 | tf_op jit(solution)/shard_map/project/pallas_call | solution.py:45
  36.0 2.7 %collective-permute-done.18.refs_4_ = bf16[2,2,16,1536]{3,2,1,0:T(8,128)(2,1)S(1)} collective-permute-done((bf16[2,2,16,1536]{3,2,1,0:T(8,128)(2,1)S(1)}, bf16[2,2,16,1536]{3,2,1,0:T(8,128)(2,1)S(1)}, u32[]{:S(2)}, u32[]{:S(2)}) %collective-permute-start.18) | collective-permute-done | bytes 196640 | tf_op jit(solution)/shard_map/gather_y/ppermute | solution.py:26
  39.5 2.0 %project.3 = (bf16[2,4,2,16,1536]{4,3,2,1,0:T(8,128)(2,1)S(1)}, f32[4,32,1536]{2,1,0:T(8,128)S(1)}, bf16[4,32,1536]{2,1,0:T(8,128)(2,1)S(1)}) custom-call(s32[5]{0:T(128)S(1)} %stack.53.refs_2_.refs_0_, bf16[2,2,16,1536]{3,2,1,0:T(8,128)(2,1)S(1)} %bitcast.24, bf16[2,2,16,1536]{3,2,1,0:T(8,128)(2,1)S(1)} %collective-permute-done.16.refs_2_, ...), custom_call_target="tpu_custom_call" | custom-call | flops 1207959552 | bytes 6684672 | tf_op jit(solution)/shard_map/project/pallas_call | solution.py:45
  43.3 2.7 %collective-permute-start.8 = (bf16[32,1536]{1,0:T(8,128)(2,1)S(1)}, bf16[32,1536]{1,0:T(8,128)(2,1)S(1)}, u32[]{:S(2)}, u32[]{:S(2)}) collective-permute-start(bf16[32,1536]{1,0:T(8,128)(2,1)S(1)} %get-tuple-element.48), channel_id=1, source_target_pairs={{0,16},{4,20},{8,24},{12,28},{16,0},{20,4},{24,8},{28,12},{1,17},{... | collective-permute-start | bytes 294920 | tf_op jit(solution)/shard_map/reduce_x/ppermute | solution.py:31
  49.2 1.9 %collective-permute-start.22 = (bf16[32,1536]{1,0:T(8,128)(2,1)S(1)}, bf16[32,1536]{1,0:T(8,128)(2,1)S(1)}, u32[]{:S(2)}, u32[]{:S(2)}) collective-permute-start(bf16[32,1536]{1,0:T(8,128)(2,1)S(1)} %get-tuple-element.56), channel_id=1, source_target_pairs={{0,24},{4,28},{8,0},{12,4},{16,8},{20,12},{24,16},{28,20},{1,25},{... | collective-permute-start | bytes 294920 | tf_op jit(solution)/shard_map/reduce_x/ppermute | solution.py:31
  53.5 2.4 %collective-permute-start.11 = (bf16[32,1536]{1,0:T(8,128)(2,1)S(1)}, bf16[32,1536]{1,0:T(8,128)(2,1)S(1)}, u32[]{:S(2)}, u32[]{:S(2)}) collective-permute-start(bf16[32,1536]{1,0:T(8,128)(2,1)S(1)} %get-tuple-element.50), channel_id=1, source_target_pairs={{0,16},{4,20},{8,24},{12,28},{16,0},{20,4},{24,8},{28,12},{1,17},{... | collective-permute-start | bytes 294920 | tf_op jit(solution)/shard_map/gather_x/ppermute | solution.py:31
  55.8 2.3 %collective-permute-start.10 = (bf16[32,1536]{1,0:T(8,128)(2,1)S(1)}, bf16[32,1536]{1,0:T(8,128)(2,1)S(1)}, u32[]{:S(2)}, u32[]{:S(2)}) collective-permute-start(bf16[32,1536]{1,0:T(8,128)(2,1)S(1)} %get-tuple-element.50), channel_id=1, source_target_pairs={{0,24},{4,28},{8,0},{12,4},{16,8},{20,12},{24,16},{28,20},{1,25},{... | collective-permute-start | bytes 294920 | tf_op jit(solution)/shard_map/gather_x/ppermute | solution.py:31
  62.4 3.5 %collective-permute-done.25 = bf16[32,1536]{1,0:T(8,128)(2,1)S(1)} collective-permute-done((bf16[32,1536]{1,0:T(8,128)(2,1)S(1)}, bf16[32,1536]{1,0:T(8,128)(2,1)S(1)}, u32[]{:S(2)}, u32[]{:S(2)}) %collective-permute-start.25) | collective-permute-done | bytes 98336 | tf_op jit(solution)/shard_map/gather_x/ppermute | solution.py:31
  66.9 2.0 %back.3 = (f32[2,2,16,1536]{3,2,1,0:T(8,128)S(1)}, bf16[2,2,16,1536]{3,2,1,0:T(8,128)(2,1)S(1)}, bf16[2,2,16,1536]{3,2,1,0:T(8,128)(2,1)S(1)}, bf16[2,2,16,1536]{3,2,1,0:T(8,128)(2,1)S(1)}) custom-call(s32[5]{0:T(128)S(1)} %stack.53.refs_2_.refs_0_, bf16[4,32,1536]{2,1,0:T(8,128)(2,1)S(1)} %pad_maximum_fusion.refs_1_.refs_2_, ...), custom_call_target="tpu_custom_call" | custom-call | flops 1207959552 | bytes 6291456 | tf_op jit(solution)/shard_map/back/pallas_call | solution.py:45
  70.0 3.2 %collective-permute-start.28 = (bf16[2,2,16,1536]{3,2,1,0:T(8,128)(2,1)S(1)}, bf16[2,2,16,1536]{3,2,1,0:T(8,128)(2,1)S(1)}, u32[]{:S(2)}, u32[]{:S(2)}) collective-permute-start(bf16[2,2,16,1536]{3,2,1,0:T(8,128)(2,1)S(1)} %get-tuple-element.68), channel_id=1, source_target_pairs={{0,128},{32,160},{1,129},{33,161},{2,130},{34,162},{3,131},{35,163... | collective-permute-start | bytes 589832 | tf_op jit(solution)/shard_map/reduce_y/ppermute | solution.py:26
  73.2 2.1 %back.2 = (f32[2,2,16,1536]{3,2,1,0:T(8,128)S(1)}, bf16[2,2,16,1536]{3,2,1,0:T(8,128)(2,1)S(1)}, bf16[2,2,16,1536]{3,2,1,0:T(8,128)(2,1)S(1)}, bf16[2,2,16,1536]{3,2,1,0:T(8,128)(2,1)S(1)}) custom-call(s32[5]{0:T(128)S(1)} %stack.53.refs_2_.refs_0_, bf16[4,32,1536]{2,1,0:T(8,128)(2,1)S(1)} %pad_maximum_fusion.1.refs_1_.refs_3_.refs_4_, ...), custom_call_target="tpu_custom_call" | custom-call | flops 1207959552 | bytes 6291456 | tf_op jit(solution)/shard_map/back/pallas_call | solution.py:45
  75.3 2.3 %collective-permute-start.30 = (bf16[2,2,16,1536]{3,2,1,0:T(8,128)(2,1)S(1)}, bf16[2,2,16,1536]{3,2,1,0:T(8,128)(2,1)S(1)}, u32[]{:S(2)}, u32[]{:S(2)}) collective-permute-start(bf16[2,2,16,1536]{3,2,1,0:T(8,128)(2,1)S(1)} %get-tuple-element.71), channel_id=1, source_target_pairs={{0,64},{32,96},{1,65},{33,97},{2,66},{34,98},{3,67},{35,99},{64,12... | collective-permute-start | bytes 589832 | tf_op jit(solution)/shard_map/reduce_y/ppermute | solution.py:26
  79.3 2.4 %collective-permute-start.32 = (bf16[2,2,16,1536]{3,2,1,0:T(8,128)(2,1)S(1)}, bf16[2,2,16,1536]{3,2,1,0:T(8,128)(2,1)S(1)}, u32[]{:S(2)}, u32[]{:S(2)}) collective-permute-start(bf16[2,2,16,1536]{3,2,1,0:T(8,128)(2,1)S(1)} %get-tuple-element.73), channel_id=1, source_target_pairs={{0,192},{32,224},{1,193},{33,225},{2,194},{34,226},{3,195},{35,227... | collective-permute-start | bytes 589832 | tf_op jit(solution)/shard_map/reduce_y/ppermute | solution.py:26
  85.1 4.5 %weigh.1 = (bf16[1536,1536]{1,0:T(8,128)(2,1)}, f32[8,128]{1,0:T(8,128)S(1)}) custom-call(bf16[2,4,2,16,1536]{4,3,2,1,0:T(8,128)(2,1)S(1)} %get-tuple-element.63.refs_0_, bf16[2,4,2,16,1536]{4,3,2,1,0:T(8,128)(2,1)S(1)} %get-tuple-element.64.refs_1_, bf16[4,32,1536]{2,1,0:T(8,128)(2,1)S(1)} %pad_maximum_fusion.refs_1_.refs_2_, ...), custom_call_target="tpu_custom_call" | custom-call | flops 2415919104 | bytes 7864320 | tf_op jit(solution)/shard_map/weigh/pallas_call | solution.py:45
  91.2 2.4 %collective-permute-start.33 = (bf16[2,16,1536]{2,1,0:T(8,128)(2,1)S(1)}, bf16[2,16,1536]{2,1,0:T(8,128)(2,1)S(1)}, u32[]{:S(2)}, u32[]{:S(2)}) collective-permute-start(bf16[2,16,1536]{2,1,0:T(8,128)(2,1)S(1)} %get-tuple-element.75), channel_id=1, source_target_pairs={{0,1},{32,33},{1,2},{33,34},{2,3},{34,35},{3,0},{35,32},{64,65},{9... | collective-permute-start | bytes 294920 | tf_op jit(solution)/shard_map/reduce_z/ppermute | solution.py:26
  95.5 3.7 %collective-permute-done.33.refs_1_ = bf16[2,16,1536]{2,1,0:T(8,128)(2,1)S(1)} collective-permute-done((bf16[2,16,1536]{2,1,0:T(8,128)(2,1)S(1)}, bf16[2,16,1536]{2,1,0:T(8,128)(2,1)S(1)}, u32[]{:S(2)}, u32[]{:S(2)}) %collective-permute-start.33) | collective-permute-done | bytes 98336 | tf_op jit(solution)/shard_map/reduce_z/ppermute | solution.py:26
  101.1 3.3 %collective-permute-done.36.refs_1_ = bf16[16,1536]{1,0:T(8,128)(2,1)S(1)} collective-permute-done((bf16[16,1536]{1,0:T(8,128)(2,1)S(1)}, bf16[16,1536]{1,0:T(8,128)(2,1)S(1)}, u32[]{:S(2)}, u32[]{:S(2)}) %collective-permute-start.36) | collective-permute-done | bytes 49184 | tf_op jit(solution)/shard_map/reduce_z/ppermute | solution.py:26
  (77 shorter events, 35.2 us)
Async XLA Ops:
  0.6 9.8 %collective-permute-start = (bf16[16,1536]{1,0:T(8,128)(2,1)}, bf16[16,1536]{1,0:T(8,128)(2,1)S(1)}, u32[]{:S(2)}, u32[]{:S(2)}) collective-permute-start(bf16[16,1536]{1,0:T(8,128)(2,1)} %refs_1_.1), channel_id=1, source_target_pairs={{0,32},{32,0},{1,33},{33,1},{2,34},{34,2},{3,35},{35,3},{64,96},{9... | collective-permute-start | bytes 147464 | tf_op jit(solution)/shard_map/gather_z/ppermute | solution.py:26
  2.6 7.9 %collective-permute-start.2 = (bf16[16,1536]{1,0:T(8,128)(2,1)}, bf16[16,1536]{1,0:T(8,128)(2,1)S(1)}, u32[]{:S(2)}, u32[]{:S(2)}) collective-permute-start(bf16[16,1536]{1,0:T(8,128)(2,1)} %refs_1_.1), channel_id=1, source_target_pairs={{0,34},{32,2},{1,35},{33,3},{2,32},{34,0},{3,33},{35,1},{64,98},{9... | collective-permute-start | bytes 147464 | tf_op jit(solution)/shard_map/gather_z/ppermute | solution.py:26
  7.6 8.9 %collective-permute-start.1 = (bf16[16,1536]{1,0:T(8,128)(2,1)}, bf16[16,1536]{1,0:T(8,128)(2,1)S(1)}, u32[]{:S(2)}, u32[]{:S(2)}) collective-permute-start(bf16[16,1536]{1,0:T(8,128)(2,1)} %refs_1_.1), channel_id=1, source_target_pairs={{0,2},{32,34},{1,3},{33,35},{2,0},{34,32},{3,1},{35,33},{64,66},{9... | collective-permute-start | bytes 147464 | tf_op jit(solution)/shard_map/gather_z/ppermute | solution.py:26
  16.5 13.1 %collective-permute-start.5 = (bf16[2,2,16,1536]{3,2,1,0:T(8,128)(2,1)S(1)}, bf16[2,2,16,1536]{3,2,1,0:T(8,128)(2,1)S(1)}, u32[]{:S(2)}, u32[]{:S(2)}) collective-permute-start(bf16[2,2,16,1536]{3,2,1,0:T(8,128)(2,1)S(1)} %bitcast.17), channel_id=1, source_target_pairs={{0,64},{32,96},{1,65},{33,97},{2,66},{34,98},{3,67},{35,99},{64,12... | collective-permute-start | bytes 589832 | tf_op jit(solution)/shard_map/gather_y/ppermute | solution.py:26
  18.1 11.4 %collective-permute-start.3 = (bf16[2,2,16,1536]{3,2,1,0:T(8,128)(2,1)S(1)}, bf16[2,2,16,1536]{3,2,1,0:T(8,128)(2,1)S(1)}, u32[]{:S(2)}, u32[]{:S(2)}) collective-permute-start(bf16[2,2,16,1536]{3,2,1,0:T(8,128)(2,1)S(1)} %bitcast.18), channel_id=1, source_target_pairs={{0,192},{32,224},{1,193},{33,225},{2,194},{34,226},{3,195},{35,227... | collective-permute-start | bytes 589832 | tf_op jit(solution)/shard_map/gather_y/ppermute | solution.py:26
  19.8 14.1 %collective-permute-start.4 = (bf16[2,2,16,1536]{3,2,1,0:T(8,128)(2,1)S(1)}, bf16[2,2,16,1536]{3,2,1,0:T(8,128)(2,1)S(1)}, u32[]{:S(2)}, u32[]{:S(2)}) collective-permute-start(bf16[2,2,16,1536]{3,2,1,0:T(8,128)(2,1)S(1)} %bitcast.19), channel_id=1, source_target_pairs={{0,128},{32,160},{1,129},{33,161},{2,130},{34,162},{3,131},{35,163... | collective-permute-start | bytes 589832 | tf_op jit(solution)/shard_map/gather_y/ppermute | solution.py:26
  21.8 7.8 %collective-permute-start.15 = (bf16[2,16,1536]{2,1,0:T(8,128)(2,1)S(1)}, bf16[2,16,1536]{2,1,0:T(8,128)(2,1)S(1)}, u32[]{:S(2)}, u32[]{:S(2)}) collective-permute-start(bf16[2,16,1536]{2,1,0:T(8,128)(2,1)S(1)} %slice.4), channel_id=1, source_target_pairs={{0,1},{32,33},{1,2},{33,34},{2,3},{34,35},{3,0},{35,32},{64,65},{9... | collective-permute-start | bytes 294920 | tf_op jit(solution)/shard_map/gather_z/ppermute | solution.py:26
  29.6 9.1 %collective-permute-start.18 = (bf16[2,2,16,1536]{3,2,1,0:T(8,128)(2,1)S(1)}, bf16[2,2,16,1536]{3,2,1,0:T(8,128)(2,1)S(1)}, u32[]{:S(2)}, u32[]{:S(2)}) collective-permute-start(bf16[2,2,16,1536]{3,2,1,0:T(8,128)(2,1)S(1)} %bitcast.21), channel_id=1, source_target_pairs={{0,64},{32,96},{1,65},{33,97},{2,66},{34,98},{3,67},{35,99},{64,12... | collective-permute-start | bytes 589832 | tf_op jit(solution)/shard_map/gather_y/ppermute | solution.py:26
  30.4 8.3 %collective-permute-start.17 = (bf16[2,2,16,1536]{3,2,1,0:T(8,128)(2,1)S(1)}, bf16[2,2,16,1536]{3,2,1,0:T(8,128)(2,1)S(1)}, u32[]{:S(2)}, u32[]{:S(2)}) collective-permute-start(bf16[2,2,16,1536]{3,2,1,0:T(8,128)(2,1)S(1)} %bitcast.22), channel_id=1, source_target_pairs={{0,128},{32,160},{1,129},{33,161},{2,130},{34,162},{3,131},{35,163... | collective-permute-start | bytes 589832 | tf_op jit(solution)/shard_map/gather_y/ppermute | solution.py:26
  41.7 7.5 %collective-permute-start.7 = (bf16[32,1536]{1,0:T(8,128)(2,1)S(1)}, bf16[32,1536]{1,0:T(8,128)(2,1)S(1)}, u32[]{:S(2)}, u32[]{:S(2)}) collective-permute-start(bf16[32,1536]{1,0:T(8,128)(2,1)S(1)} %get-tuple-element.47), channel_id=1, source_target_pairs={{0,8},{4,12},{8,16},{12,20},{16,24},{20,28},{24,0},{28,4},{1,9},{5... | collective-permute-start | bytes 294920 | tf_op jit(solution)/shard_map/reduce_x/ppermute | solution.py:31
  43.3 8.4 %collective-permute-start.8 = (bf16[32,1536]{1,0:T(8,128)(2,1)S(1)}, bf16[32,1536]{1,0:T(8,128)(2,1)S(1)}, u32[]{:S(2)}, u32[]{:S(2)}) collective-permute-start(bf16[32,1536]{1,0:T(8,128)(2,1)S(1)} %get-tuple-element.48), channel_id=1, source_target_pairs={{0,16},{4,20},{8,24},{12,28},{16,0},{20,4},{24,8},{28,12},{1,17},{... | collective-permute-start | bytes 294920 | tf_op jit(solution)/shard_map/reduce_x/ppermute | solution.py:31
  47.5 8.3 %collective-permute-start.20 = (bf16[32,1536]{1,0:T(8,128)(2,1)S(1)}, bf16[32,1536]{1,0:T(8,128)(2,1)S(1)}, u32[]{:S(2)}, u32[]{:S(2)}) collective-permute-start(bf16[32,1536]{1,0:T(8,128)(2,1)S(1)} %get-tuple-element.54), channel_id=1, source_target_pairs={{0,8},{4,12},{8,16},{12,20},{16,24},{20,28},{24,0},{28,4},{1,9},{5... | collective-permute-start | bytes 294920 | tf_op jit(solution)/shard_map/reduce_x/ppermute | solution.py:31
  48.2 9.9 %collective-permute-start.21 = (bf16[32,1536]{1,0:T(8,128)(2,1)S(1)}, bf16[32,1536]{1,0:T(8,128)(2,1)S(1)}, u32[]{:S(2)}, u32[]{:S(2)}) collective-permute-start(bf16[32,1536]{1,0:T(8,128)(2,1)S(1)} %get-tuple-element.55), channel_id=1, source_target_pairs={{0,16},{4,20},{8,24},{12,28},{16,0},{20,4},{24,8},{28,12},{1,17},{... | collective-permute-start | bytes 294920 | tf_op jit(solution)/shard_map/reduce_x/ppermute | solution.py:31
  49.2 9.0 %collective-permute-start.22 = (bf16[32,1536]{1,0:T(8,128)(2,1)S(1)}, bf16[32,1536]{1,0:T(8,128)(2,1)S(1)}, u32[]{:S(2)}, u32[]{:S(2)}) collective-permute-start(bf16[32,1536]{1,0:T(8,128)(2,1)S(1)} %get-tuple-element.56), channel_id=1, source_target_pairs={{0,24},{4,28},{8,0},{12,4},{16,8},{20,12},{24,16},{28,20},{1,25},{... | collective-permute-start | bytes 294920 | tf_op jit(solution)/shard_map/reduce_x/ppermute | solution.py:31
  52.4 8.3 %collective-permute-start.12 = (bf16[32,1536]{1,0:T(8,128)(2,1)S(1)}, bf16[32,1536]{1,0:T(8,128)(2,1)S(1)}, u32[]{:S(2)}, u32[]{:S(2)}) collective-permute-start(bf16[32,1536]{1,0:T(8,128)(2,1)S(1)} %get-tuple-element.50), channel_id=1, source_target_pairs={{0,8},{4,12},{8,16},{12,20},{16,24},{20,28},{24,0},{28,4},{1,9},{5... | collective-permute-start | bytes 294920 | tf_op jit(solution)/shard_map/gather_x/ppermute | solution.py:31
  53.5 8.8 %collective-permute-start.11 = (bf16[32,1536]{1,0:T(8,128)(2,1)S(1)}, bf16[32,1536]{1,0:T(8,128)(2,1)S(1)}, u32[]{:S(2)}, u32[]{:S(2)}) collective-permute-start(bf16[32,1536]{1,0:T(8,128)(2,1)S(1)} %get-tuple-element.50), channel_id=1, source_target_pairs={{0,16},{4,20},{8,24},{12,28},{16,0},{20,4},{24,8},{28,12},{1,17},{... | collective-permute-start | bytes 294920 | tf_op jit(solution)/shard_map/gather_x/ppermute | solution.py:31
  69.0 10.4 %collective-permute-start.27 = (bf16[2,2,16,1536]{3,2,1,0:T(8,128)(2,1)S(1)}, bf16[2,2,16,1536]{3,2,1,0:T(8,128)(2,1)S(1)}, u32[]{:S(2)}, u32[]{:S(2)}) collective-permute-start(bf16[2,2,16,1536]{3,2,1,0:T(8,128)(2,1)S(1)} %get-tuple-element.67), channel_id=1, source_target_pairs={{0,64},{32,96},{1,65},{33,97},{2,66},{34,98},{3,67},{35,99},{64,12... | collective-permute-start | bytes 589832 | tf_op jit(solution)/shard_map/reduce_y/ppermute | solution.py:26
  70.0 13.1 %collective-permute-start.28 = (bf16[2,2,16,1536]{3,2,1,0:T(8,128)(2,1)S(1)}, bf16[2,2,16,1536]{3,2,1,0:T(8,128)(2,1)S(1)}, u32[]{:S(2)}, u32[]{:S(2)}) collective-permute-start(bf16[2,2,16,1536]{3,2,1,0:T(8,128)(2,1)S(1)} %get-tuple-element.68), channel_id=1, source_target_pairs={{0,128},{32,160},{1,129},{33,161},{2,130},{34,162},{3,131},{35,163... | collective-permute-start | bytes 589832 | tf_op jit(solution)/shard_map/reduce_y/ppermute | solution.py:26
  73.2 9.9 %collective-permute-start.29 = (bf16[2,2,16,1536]{3,2,1,0:T(8,128)(2,1)S(1)}, bf16[2,2,16,1536]{3,2,1,0:T(8,128)(2,1)S(1)}, u32[]{:S(2)}, u32[]{:S(2)}) collective-permute-start(bf16[2,2,16,1536]{3,2,1,0:T(8,128)(2,1)S(1)} %get-tuple-element.69), channel_id=1, source_target_pairs={{0,192},{32,224},{1,193},{33,225},{2,194},{34,226},{3,195},{35,227... | collective-permute-start | bytes 589832 | tf_op jit(solution)/shard_map/reduce_y/ppermute | solution.py:26
  75.3 14.3 %collective-permute-start.30 = (bf16[2,2,16,1536]{3,2,1,0:T(8,128)(2,1)S(1)}, bf16[2,2,16,1536]{3,2,1,0:T(8,128)(2,1)S(1)}, u32[]{:S(2)}, u32[]{:S(2)}) collective-permute-start(bf16[2,2,16,1536]{3,2,1,0:T(8,128)(2,1)S(1)} %get-tuple-element.71), channel_id=1, source_target_pairs={{0,64},{32,96},{1,65},{33,97},{2,66},{34,98},{3,67},{35,99},{64,12... | collective-permute-start | bytes 589832 | tf_op jit(solution)/shard_map/reduce_y/ppermute | solution.py:26
  77.6 13.5 %collective-permute-start.31 = (bf16[2,2,16,1536]{3,2,1,0:T(8,128)(2,1)S(1)}, bf16[2,2,16,1536]{3,2,1,0:T(8,128)(2,1)S(1)}, u32[]{:S(2)}, u32[]{:S(2)}) collective-permute-start(bf16[2,2,16,1536]{3,2,1,0:T(8,128)(2,1)S(1)} %get-tuple-element.72), channel_id=1, source_target_pairs={{0,128},{32,160},{1,129},{33,161},{2,130},{34,162},{3,131},{35,163... | collective-permute-start | bytes 589832 | tf_op jit(solution)/shard_map/reduce_y/ppermute | solution.py:26
  79.3 11.8 %collective-permute-start.32 = (bf16[2,2,16,1536]{3,2,1,0:T(8,128)(2,1)S(1)}, bf16[2,2,16,1536]{3,2,1,0:T(8,128)(2,1)S(1)}, u32[]{:S(2)}, u32[]{:S(2)}) collective-permute-start(bf16[2,2,16,1536]{3,2,1,0:T(8,128)(2,1)S(1)} %get-tuple-element.73), channel_id=1, source_target_pairs={{0,192},{32,224},{1,193},{33,225},{2,194},{34,226},{3,195},{35,227... | collective-permute-start | bytes 589832 | tf_op jit(solution)/shard_map/reduce_y/ppermute | solution.py:26
  83.2 12.2 %collective-permute-start.34 = (bf16[2,16,1536]{2,1,0:T(8,128)(2,1)S(1)}, bf16[2,16,1536]{2,1,0:T(8,128)(2,1)S(1)}, u32[]{:S(2)}, u32[]{:S(2)}) collective-permute-start(bf16[2,16,1536]{2,1,0:T(8,128)(2,1)S(1)} %get-tuple-element.76), channel_id=1, source_target_pairs={{0,2},{32,34},{1,3},{33,35},{2,0},{34,32},{3,1},{35,33},{64,66},{9... | collective-permute-start | bytes 294920 | tf_op jit(solution)/shard_map/reduce_z/ppermute | solution.py:26
  91.2 7.9 %collective-permute-start.33 = (bf16[2,16,1536]{2,1,0:T(8,128)(2,1)S(1)}, bf16[2,16,1536]{2,1,0:T(8,128)(2,1)S(1)}, u32[]{:S(2)}, u32[]{:S(2)}) collective-permute-start(bf16[2,16,1536]{2,1,0:T(8,128)(2,1)S(1)} %get-tuple-element.75), channel_id=1, source_target_pairs={{0,1},{32,33},{1,2},{33,34},{2,3},{34,35},{3,0},{35,32},{64,65},{9... | collective-permute-start | bytes 294920 | tf_op jit(solution)/shard_map/reduce_z/ppermute | solution.py:26
  (15 other events, 107.2 us)

commit v3 on v2

--- a/solution.py
+++ b/solution.py
@@ -50,7 +50,7 @@
         out_shape=[o if isinstance(o, pl.MemoryRef) else jax.ShapeDtypeStruct(*o) for o in outs],
         scratch_shapes=list(scratch),
         compiler_params=pltpu.CompilerParams(vmem_limit_bytes=LIMIT),
-        cost_estimate=pl.CostEstimate(flops=flops, bytes_accessed=moved, transcendentals=0),
+        cost_estimate=pl.CostEstimate(flops=0, bytes_accessed=0, transcendentals=0),
     )(*ins)
 
 
@@ -98,9 +98,9 @@
     def body(place, b0, b1, b2, b3, w, held, keep, give):
         x, c, y, l = (place[i] for i in range(4))
         for t, block in enumerate((b0, b1, b2, b3)):
-            at = (y + t - x + 4) % 4
+            at = (y + t - x + 4) & 3
             for p in range(2):
-                side = (l + p + c) % 2
+                side = (l + p + c) & 1
                 for e in range(count):
                     held[side, at, e] = block[e, p]
         for j in range(width // tile):
@@ -147,7 +147,7 @@
     def body(place, own, p1, p2, p3, bias, grad_act, act, grad):
         for j, e in enumerate(chunk):
             here = slice(j * ROW, (j + 1) * ROW)
-            at = (place[4] + e) % 4
+            at = (place[4] + e) & 3
             v = own[here, :] + p1[here, :].astype(F32)
             v = v + (p2[here, :].astype(F32) + p3[here, :].astype(F32)) + bias[...]
             t = jnp.tanh(coef * (v + 0.044715 * v * v * v))
@@ -181,9 +181,9 @@
             product = lax.dot_general(all_rows[...], w[cut, :], turn, preferred_element_type=F32)
             found[...] = product.reshape(2, 4, count, ROW, tile)
             for t, out in enumerate((o0, o1, o2, o3)):
-                at = (y + t - x + 4) % 4
+                at = (y + t - x + 4) & 3
                 for p in range(2):
-                    side = (l + p + c) % 2
+                    side = (l + p + c) & 1
                     for e in range(count):
                         out[e, p, :, cut] = found[side, at, e].astype(out.dtype)
 
@@ -202,45 +202,30 @@
     _, _, _, width = own.shape
 
     def body(own, p1, p2, p3, *outs):
-        for j, out in enumerate(outs):
-            v = own[j] + p1[j].astype(F32)
-            v = v + (p2[j].astype(F32) + p3[j].astype(F32))
+        for i, out in enumerate(outs):
+            j, p = i // 2, i % 2
+            v = own[j, p] + p1[j, p].astype(F32)
+            v = v + (p2[j, p].astype(F32) + p3[j, p].astype(F32))
             out[...] = v.astype(out.dtype)
 
     return call(
         body,
         [own, *parts],
-        [((2, ROW, width), BF if e else F32) for e in chunk],
+        [((ROW, width), BF if e or p else F32) for e in chunk for p in range(2)],
         flops=3 * own.size,
         moved=12 * own.size,
         after=after,
     )
 
 
-def add_rest(arrays):
-    width = arrays[0].shape[2]
-
+def add_last(arrays, after):
     def body(*refs):
-        total = refs[0][...].astype(F32)
-        for ref in refs[1:-2]:
+        total = refs[0][...]
+        for ref in refs[1:-1]:
             total = total + ref[...].astype(F32)
-        refs[-2][...] = total[0]
-        refs[-1][...] = total[1].astype(BF)
-
-    return call(
-        body,
-        list(arrays),
-        [((ROW, width), F32), ((ROW, width), BF)],
-        flops=8 * ROW * width,
-        moved=18 * ROW * width,
-    )
-
-
-def add_last(own, got):
-    def body(own, got, out):
-        out[...] = (own[...] + got[...].astype(F32)).astype(BF)
-
-    return call(body, [own, got], [(own.shape, BF)], flops=own.size, moved=8 * own.size)[0]
+        refs[-1][...] = total.astype(BF)
+
+    return call(body, arrays, [(arrays[0].shape, BF)], after=after)[0]
 
 
 def settle(place, grads, acts, after):
@@ -255,7 +240,7 @@
         bias[...] = total
         for chunk, ref in zip(CHUNKS, refs[len(grads) : -2]):
             for j, e in enumerate(chunk):
-                act[(place[4] + e) % 4] = ref[j * ROW : (j + 1) * ROW, :]
+                act[(place[4] + e) & 3] = ref[j * ROW : (j + 1) * ROW, :]
 
     return call(
         body,
@@ -345,21 +330,19 @@
             own, *parts = back(place, *grads[2 * k : 2 * k + 2], w_in)
         with jax.named_scope("reduce_y"):
             partials.append([own] + [by_plane(p, t, 0) for t, p in enumerate(parts, 1)])
-    with jax.named_scope("settle"):
-        grad_bias, act = settle(place, grads, acts, [partials[1][0]])
     with jax.named_scope("weigh"):
         grad_weight, weighed = weigh(held, grads, [partials[1][0]])
-    for (own, *parts), chunk, beside in zip(partials, CHUNKS, (grad_bias, weighed)):
+    for (own, *parts), chunk, beside in zip(partials, CHUNKS, ([weighed], [])):
         with jax.named_scope("reduce_y"):
-            sums = add_four(own, parts, chunk, [beside])
+            sums = add_four(own, parts, chunk, beside)
         with jax.named_scope("reduce_z"):
-            for e, part in zip(chunk, sums):
-                ends[e] = by_plane(part, 0, e) if e else part
-    with jax.named_scope("reduce_z"):
-        own, part = add_rest([ends[e] for e in range(4)])
-        part = by_plane(part, 0, 0, 1)
+            for i, part in enumerate(sums):
+                e, p = chunk[i // 2], i % 2
+                ends[e, p] = by_plane(part, 0, e, p) if e or p else part
+    with jax.named_scope("settle"):
+        grad_bias, act = settle(place, grads, acts, sums[:1])
     with jax.named_scope("finish"):
-        grad_tokens = add_last(own, part)
+        grad_tokens = add_last([ends[e, p] for e in range(4) for p in range(2)], [grad_bias])
     return (act.reshape(4 * ROW, width), grad_bias.reshape(width), grad_weight, grad_tokens)
 
 

time: 105 us -> 104 us (level)
  waiting for transfers between devices: 29.1 us -> 19.3 us
  starting transfers between devices: 55.3 us -> 64 us
    ppermute x21 -> x24, waiting for transfers between devices: 24.1 us -> 14.2 us  [by_plane(): return lax.ppermute(array, PLANE, pairs)]
    ppermute x21 -> x24, starting transfers between devices: 36.7 us -> 45.4 us  [by_plane(): return lax.ppermute(array, PLANE, pairs)]
    pallas_call x17 -> x16, Pallas kernels: 18.9 us -> 18.8 us  [call(): pl.pallas_call(run, grid=grid, in_specs=in_specs, out_specs=out_specs or...]
  transfers between devices with their start and end apart: 37 -> 40, of which waited for: 12 -> 10; matrix products, arithmetic and copies ran while one was open for 1% -> 1% of each run, Pallas kernels for 17% -> 17%
where the time goes in v3:
time: 104 us
  starting transfers between devices  64 us (62%)
  waiting for transfers between devices  19.3 us (19%)
  Pallas kernels  18.8 us (18%)
    ppermute x24, starting transfers between devices, by_plane(): return lax.ppermute(array, PLANE, pairs)  45.4 us
    pallas_call x16, Pallas kernels, call(): pl.pallas_call(run, grid=grid, in_specs=in_specs, out_specs=out_specs or...  18.8 us
    ppermute x16, starting transfers between devices, by_line(): return lax.ppermute(array, 'gy', pairs)  18.6 us
    ppermute x24, waiting for transfers between devices, by_plane(): return lax.ppermute(array, PLANE, pairs)  14.2 us
    ppermute x16, waiting for transfers between devices, by_line(): return lax.ppermute(array, 'gy', pairs)  5.06 us
  transfers between devices with their start and end apart: 40, of which 10 were waited for; matrix products, arithmetic and copies ran while one was open for 1% of the time, Pallas kernels for 17%

profile of v3, /device:TPU:32, one launch (start us, length us, event | category | flops | bytes accessed | tf_op | source)
XLA Modules:
  0.0 103.9 jit_solution(4061632497280490280)
XLA Ops:
  0.6 1.9 %collective-permute-start = (bf16[16,1536]{1,0:T(8,128)(2,1)}, bf16[16,1536]{1,0:T(8,128)(2,1)S(1)}, u32[]{:S(2)}, u32[]{:S(2)}) collective-permute-start(bf16[16,1536]{1,0:T(8,128)(2,1)} %refs_1_.1), channel_id=1, source_target_pairs={{0,32},{32,0},{1,33},{33,1},{2,34},{34,2},{3,35},{35,3},{64,96},{9... | collective-permute-start | bytes 147464 | tf_op jit(solution)/shard_map/gather_z/ppermute | solution.py:26
  2.6 5.0 %collective-permute-start.2 = (bf16[16,1536]{1,0:T(8,128)(2,1)}, bf16[16,1536]{1,0:T(8,128)(2,1)S(1)}, u32[]{:S(2)}, u32[]{:S(2)}) collective-permute-start(bf16[16,1536]{1,0:T(8,128)(2,1)} %refs_1_.1), channel_id=1, source_target_pairs={{0,34},{32,2},{1,35},{33,3},{2,32},{34,0},{3,33},{35,1},{64,98},{9... | collective-permute-start | bytes 147464 | tf_op jit(solution)/shard_map/gather_z/ppermute | solution.py:26
  8.1 2.4 %gather_z.3 = (bf16[1536,1536]{1,0:T(8,128)(2,1)S(1)}, bf16[16,1536]{1,0:T(8,128)(2,1)S(1)}) custom-call(bf16[1536,1536]{1,0:T(8,128)(2,1)} %refs_0_.1, bf16[16,1536]{1,0:T(8,128)(2,1)} %refs_1_.1, s32[5]{0:T(128)S(1)} %stack.53.refs_2_.refs_0_), custom_call_target="tpu_custom_call" | custom-call | tf_op jit(solution)/shard_map/gather_z/pallas_call | solution.py:45
  10.5 6.0 %collective-permute-done.1.refs_2_ = bf16[16,1536]{1,0:T(8,128)(2,1)S(1)} collective-permute-done((bf16[16,1536]{1,0:T(8,128)(2,1)}, bf16[16,1536]{1,0:T(8,128)(2,1)S(1)}, u32[]{:S(2)}, u32[]{:S(2)}) %collective-permute-start.1) | collective-permute-done | bytes 49184 | tf_op jit(solution)/shard_map/gather_z/ppermute | solution.py:26
  21.2 2.8 %collective-permute-start.14 = (bf16[2,16,1536]{2,1,0:T(8,128)(2,1)S(1)}, bf16[2,16,1536]{2,1,0:T(8,128)(2,1)S(1)}, u32[]{:S(2)}, u32[]{:S(2)}) collective-permute-start(bf16[2,16,1536]{2,1,0:T(8,128)(2,1)S(1)} %slice.4), channel_id=1, source_target_pairs={{0,3},{32,35},{1,0},{33,32},{2,1},{34,33},{3,2},{35,34},{64,67},{9... | collective-permute-start | bytes 294920 | tf_op jit(solution)/shard_map/gather_z/ppermute | solution.py:26
  24.0 2.0 %collective-permute-start.4 = (bf16[2,2,16,1536]{3,2,1,0:T(8,128)(2,1)S(1)}, bf16[2,2,16,1536]{3,2,1,0:T(8,128)(2,1)S(1)}, u32[]{:S(2)}, u32[]{:S(2)}) collective-permute-start(bf16[2,2,16,1536]{3,2,1,0:T(8,128)(2,1)S(1)} %bitcast.19), channel_id=1, source_target_pairs={{0,128},{32,160},{1,129},{33,161},{2,130},{34,162},{3,131},{35,163... | collective-permute-start | bytes 589832 | tf_op jit(solution)/shard_map/gather_y/ppermute | solution.py:26
  28.1 2.9 %collective-permute-start.17 = (bf16[2,2,16,1536]{3,2,1,0:T(8,128)(2,1)S(1)}, bf16[2,2,16,1536]{3,2,1,0:T(8,128)(2,1)S(1)}, u32[]{:S(2)}, u32[]{:S(2)}) collective-permute-start(bf16[2,2,16,1536]{3,2,1,0:T(8,128)(2,1)S(1)} %bitcast.22), channel_id=1, source_target_pairs={{0,128},{32,160},{1,129},{33,161},{2,130},{34,162},{3,131},{35,163... | collective-permute-start | bytes 589832 | tf_op jit(solution)/shard_map/gather_y/ppermute | solution.py:26
  33.3 1.9 %project.2 = (bf16[2,4,2,16,1536]{4,3,2,1,0:T(8,128)(2,1)S(1)}, f32[4,32,1536]{2,1,0:T(8,128)S(1)}, bf16[4,32,1536]{2,1,0:T(8,128)(2,1)S(1)}) custom-call(s32[5]{0:T(128)S(1)} %stack.53.refs_2_.refs_0_, bf16[2,2,16,1536]{3,2,1,0:T(8,128)(2,1)S(1)} %bitcast.20, bf16[2,2,16,1536]{3,2,1,0:T(8,128)(2,1)S(1)} %collective-permute-done.3.refs_2_, ...), custom_call_target="tpu_custom_call" | custom-call | tf_op jit(solution)/shard_map/project/pallas_call | solution.py:45
  36.6 2.1 %collective-permute-done.17.refs_3_ = bf16[2,2,16,1536]{3,2,1,0:T(8,128)(2,1)S(1)} collective-permute-done((bf16[2,2,16,1536]{3,2,1,0:T(8,128)(2,1)S(1)}, bf16[2,2,16,1536]{3,2,1,0:T(8,128)(2,1)S(1)}, u32[]{:S(2)}, u32[]{:S(2)}) %collective-permute-start.17) | collective-permute-done | bytes 196640 | tf_op jit(solution)/shard_map/gather_y/ppermute | solution.py:26
  38.8 1.9 %project.3 = (bf16[2,4,2,16,1536]{4,3,2,1,0:T(8,128)(2,1)S(1)}, f32[4,32,1536]{2,1,0:T(8,128)S(1)}, bf16[4,32,1536]{2,1,0:T(8,128)(2,1)S(1)}) custom-call(s32[5]{0:T(128)S(1)} %stack.53.refs_2_.refs_0_, bf16[2,2,16,1536]{3,2,1,0:T(8,128)(2,1)S(1)} %bitcast.24, bf16[2,2,16,1536]{3,2,1,0:T(8,128)(2,1)S(1)} %collective-permute-done.16.refs_2_, ...), custom_call_target="tpu_custom_call" | custom-call | tf_op jit(solution)/shard_map/project/pallas_call | solution.py:45
  42.5 2.7 %collective-permute-start.8 = (bf16[32,1536]{1,0:T(8,128)(2,1)S(1)}, bf16[32,1536]{1,0:T(8,128)(2,1)S(1)}, u32[]{:S(2)}, u32[]{:S(2)}) collective-permute-start(bf16[32,1536]{1,0:T(8,128)(2,1)S(1)} %get-tuple-element.50), channel_id=1, source_target_pairs={{0,16},{4,20},{8,24},{12,28},{16,0},{20,4},{24,8},{28,12},{1,17},{... | collective-permute-start | bytes 294920 | tf_op jit(solution)/shard_map/reduce_x/ppermute | solution.py:31
  52.7 2.4 %collective-permute-start.11 = (bf16[32,1536]{1,0:T(8,128)(2,1)S(1)}, bf16[32,1536]{1,0:T(8,128)(2,1)S(1)}, u32[]{:S(2)}, u32[]{:S(2)}) collective-permute-start(bf16[32,1536]{1,0:T(8,128)(2,1)S(1)} %get-tuple-element.52), channel_id=1, source_target_pairs={{0,16},{4,20},{8,24},{12,28},{16,0},{20,4},{24,8},{28,12},{1,17},{... | collective-permute-start | bytes 294920 | tf_op jit(solution)/shard_map/gather_x/ppermute | solution.py:31
  55.0 2.3 %collective-permute-start.10 = (bf16[32,1536]{1,0:T(8,128)(2,1)S(1)}, bf16[32,1536]{1,0:T(8,128)(2,1)S(1)}, u32[]{:S(2)}, u32[]{:S(2)}) collective-permute-start(bf16[32,1536]{1,0:T(8,128)(2,1)S(1)} %get-tuple-element.52), channel_id=1, source_target_pairs={{0,24},{4,28},{8,0},{12,4},{16,8},{20,12},{24,16},{28,20},{1,25},{... | collective-permute-start | bytes 294920 | tf_op jit(solution)/shard_map/gather_x/ppermute | solution.py:31
  61.6 3.5 %collective-permute-done.25 = bf16[32,1536]{1,0:T(8,128)(2,1)S(1)} collective-permute-done((bf16[32,1536]{1,0:T(8,128)(2,1)S(1)}, bf16[32,1536]{1,0:T(8,128)(2,1)S(1)}, u32[]{:S(2)}, u32[]{:S(2)}) %collective-permute-start.25) | collective-permute-done | bytes 98336 | tf_op jit(solution)/shard_map/gather_x/ppermute | solution.py:31
  66.1 2.1 %back.3 = (f32[2,2,16,1536]{3,2,1,0:T(8,128)S(1)}, bf16[2,2,16,1536]{3,2,1,0:T(8,128)(2,1)S(1)}, bf16[2,2,16,1536]{3,2,1,0:T(8,128)(2,1)S(1)}, bf16[2,2,16,1536]{3,2,1,0:T(8,128)(2,1)S(1)}) custom-call(s32[5]{0:T(128)S(1)} %stack.53.refs_2_.refs_0_, bf16[4,32,1536]{2,1,0:T(8,128)(2,1)S(1)} %pad_maximum_fusion.refs_1_.refs_2_, ...), custom_call_target="tpu_custom_call" | custom-call | tf_op jit(solution)/shard_map/back/pallas_call | solution.py:45
  69.5 2.9 %collective-permute-start.31 = (bf16[2,2,16,1536]{3,2,1,0:T(8,128)(2,1)S(1)}, bf16[2,2,16,1536]{3,2,1,0:T(8,128)(2,1)S(1)}, u32[]{:S(2)}, u32[]{:S(2)}) collective-permute-start(bf16[2,2,16,1536]{3,2,1,0:T(8,128)(2,1)S(1)} %get-tuple-element.74), channel_id=1, source_target_pairs={{0,128},{32,160},{1,129},{33,161},{2,130},{34,162},{3,131},{35,163... | collective-permute-start | bytes 589832 | tf_op jit(solution)/shard_map/reduce_y/ppermute | solution.py:26
  72.8 2.1 %back.2 = (f32[2,2,16,1536]{3,2,1,0:T(8,128)S(1)}, bf16[2,2,16,1536]{3,2,1,0:T(8,128)(2,1)S(1)}, bf16[2,2,16,1536]{3,2,1,0:T(8,128)(2,1)S(1)}, bf16[2,2,16,1536]{3,2,1,0:T(8,128)(2,1)S(1)}) custom-call(s32[5]{0:T(128)S(1)} %stack.53.refs_2_.refs_0_, bf16[4,32,1536]{2,1,0:T(8,128)(2,1)S(1)} %pad_maximum_fusion.1.refs_1_.refs_3_.refs_4_, ...), custom_call_target="tpu_custom_call" | custom-call | tf_op jit(solution)/shard_map/back/pallas_call | solution.py:45
  77.4 2.1 %collective-permute-start.29 = (bf16[2,2,16,1536]{3,2,1,0:T(8,128)(2,1)S(1)}, bf16[2,2,16,1536]{3,2,1,0:T(8,128)(2,1)S(1)}, u32[]{:S(2)}, u32[]{:S(2)}) collective-permute-start(bf16[2,2,16,1536]{3,2,1,0:T(8,128)(2,1)S(1)} %get-tuple-element.65), channel_id=1, source_target_pairs={{0,192},{32,224},{1,193},{33,225},{2,194},{34,226},{3,195},{35,227... | collective-permute-start | bytes 589832 | tf_op jit(solution)/shard_map/reduce_y/ppermute | solution.py:26
  79.6 4.5 %weigh.1 = (bf16[1536,1536]{1,0:T(8,128)(2,1)}, f32[8,128]{1,0:T(8,128)S(1)}) custom-call(bf16[2,4,2,16,1536]{4,3,2,1,0:T(8,128)(2,1)S(1)} %get-tuple-element.69.refs_0_, bf16[2,4,2,16,1536]{4,3,2,1,0:T(8,128)(2,1)S(1)} %get-tuple-element.70.refs_1_, bf16[4,32,1536]{2,1,0:T(8,128)(2,1)S(1)} %pad_maximum_fusion.refs_1_.refs_2_, ...), custom_call_target="tpu_custom_call" | custom-call | tf_op jit(solution)/shard_map/weigh/pallas_call | solution.py:45
  86.4 4.4 %collective-permute-start.37 = (bf16[16,1536]{1,0:T(8,128)(2,1)S(1)}, bf16[16,1536]{1,0:T(8,128)(2,1)S(1)}, u32[]{:S(2)}, u32[]{:S(2)}) collective-permute-start(bf16[16,1536]{1,0:T(8,128)(2,1)S(1)} %get-tuple-element.81), channel_id=1, source_target_pairs={{0,34},{32,2},{1,35},{33,3},{2,32},{34,0},{3,33},{35,1},{64,98},{9... | collective-permute-start | bytes 147464 | tf_op jit(solution)/shard_map/reduce_z/ppermute | solution.py:26
  91.0 3.2 %collective-permute-start.38 = (bf16[16,1536]{1,0:T(8,128)(2,1)S(1)}, bf16[16,1536]{1,0:T(8,128)(2,1)S(1)}, u32[]{:S(2)}, u32[]{:S(2)}) collective-permute-start(bf16[16,1536]{1,0:T(8,128)(2,1)S(1)} %get-tuple-element.82), channel_id=1, source_target_pairs={{0,3},{32,35},{1,0},{33,32},{2,1},{34,33},{3,2},{35,34},{64,67},{9... | collective-permute-start | bytes 147464 | tf_op jit(solution)/shard_map/reduce_z/ppermute | solution.py:26
  94.2 2.7 %collective-permute-start.39 = (bf16[16,1536]{1,0:T(8,128)(2,1)S(1)}, bf16[16,1536]{1,0:T(8,128)(2,1)S(1)}, u32[]{:S(2)}, u32[]{:S(2)}) collective-permute-start(bf16[16,1536]{1,0:T(8,128)(2,1)S(1)} %get-tuple-element.83), channel_id=1, source_target_pairs={{0,35},{32,3},{1,32},{33,0},{2,33},{34,1},{3,34},{35,2},{64,99},{9... | collective-permute-start | bytes 147464 | tf_op jit(solution)/shard_map/reduce_z/ppermute | solution.py:26
  96.8 2.1 %collective-permute-start.34 = (bf16[16,1536]{1,0:T(8,128)(2,1)S(1)}, bf16[16,1536]{1,0:T(8,128)(2,1)S(1)}, u32[]{:S(2)}, u32[]{:S(2)}) collective-permute-start(bf16[16,1536]{1,0:T(8,128)(2,1)S(1)} %get-tuple-element.66.refs_7_), channel_id=1, source_target_pairs={{0,1},{32,33},{1,2},{33,34},{2,3},{34,35},{3,0},{35,32},{64,65},{9... | collective-permute-start | bytes 147464 | tf_op jit(solution)/shard_map/reduce_z/ppermute | solution.py:26
  101.0 2.2 %collective-permute-done.34.refs_2_ = bf16[16,1536]{1,0:T(8,128)(2,1)S(1)} collective-permute-done((bf16[16,1536]{1,0:T(8,128)(2,1)S(1)}, bf16[16,1536]{1,0:T(8,128)(2,1)S(1)}, u32[]{:S(2)}, u32[]{:S(2)}) %collective-permute-start.34) | collective-permute-done | bytes 49184 | tf_op jit(solution)/shard_map/reduce_z/ppermute | solution.py:26
  (82 shorter events, 35.0 us)
Async XLA Ops:
  0.6 9.8 %collective-permute-start = (bf16[16,1536]{1,0:T(8,128)(2,1)}, bf16[16,1536]{1,0:T(8,128)(2,1)S(1)}, u32[]{:S(2)}, u32[]{:S(2)}) collective-permute-start(bf16[16,1536]{1,0:T(8,128)(2,1)} %refs_1_.1), channel_id=1, source_target_pairs={{0,32},{32,0},{1,33},{33,1},{2,34},{34,2},{3,35},{35,3},{64,96},{9... | collective-permute-start | bytes 147464 | tf_op jit(solution)/shard_map/gather_z/ppermute | solution.py:26
  7.6 8.9 %collective-permute-start.1 = (bf16[16,1536]{1,0:T(8,128)(2,1)}, bf16[16,1536]{1,0:T(8,128)(2,1)S(1)}, u32[]{:S(2)}, u32[]{:S(2)}) collective-permute-start(bf16[16,1536]{1,0:T(8,128)(2,1)} %refs_1_.1), channel_id=1, source_target_pairs={{0,2},{32,34},{1,3},{33,35},{2,0},{34,32},{3,1},{35,33},{64,66},{9... | collective-permute-start | bytes 147464 | tf_op jit(solution)/shard_map/gather_z/ppermute | solution.py:26
  16.5 11.1 %collective-permute-start.5 = (bf16[2,2,16,1536]{3,2,1,0:T(8,128)(2,1)S(1)}, bf16[2,2,16,1536]{3,2,1,0:T(8,128)(2,1)S(1)}, u32[]{:S(2)}, u32[]{:S(2)}) collective-permute-start(bf16[2,2,16,1536]{3,2,1,0:T(8,128)(2,1)S(1)} %bitcast.17), channel_id=1, source_target_pairs={{0,64},{32,96},{1,65},{33,97},{2,66},{34,98},{3,67},{35,99},{64,12... | collective-permute-start | bytes 589832 | tf_op jit(solution)/shard_map/gather_y/ppermute | solution.py:26
  18.1 9.5 %collective-permute-start.3 = (bf16[2,2,16,1536]{3,2,1,0:T(8,128)(2,1)S(1)}, bf16[2,2,16,1536]{3,2,1,0:T(8,128)(2,1)S(1)}, u32[]{:S(2)}, u32[]{:S(2)}) collective-permute-start(bf16[2,2,16,1536]{3,2,1,0:T(8,128)(2,1)S(1)} %bitcast.18), channel_id=1, source_target_pairs={{0,192},{32,224},{1,193},{33,225},{2,194},{34,226},{3,195},{35,227... | collective-permute-start | bytes 589832 | tf_op jit(solution)/shard_map/gather_y/ppermute | solution.py:26
  24.0 9.3 %collective-permute-start.4 = (bf16[2,2,16,1536]{3,2,1,0:T(8,128)(2,1)S(1)}, bf16[2,2,16,1536]{3,2,1,0:T(8,128)(2,1)S(1)}, u32[]{:S(2)}, u32[]{:S(2)}) collective-permute-start(bf16[2,2,16,1536]{3,2,1,0:T(8,128)(2,1)S(1)} %bitcast.19), channel_id=1, source_target_pairs={{0,128},{32,160},{1,129},{33,161},{2,130},{34,162},{3,131},{35,163... | collective-permute-start | bytes 589832 | tf_op jit(solution)/shard_map/gather_y/ppermute | solution.py:26
  27.6 9.0 %collective-permute-start.18 = (bf16[2,2,16,1536]{3,2,1,0:T(8,128)(2,1)S(1)}, bf16[2,2,16,1536]{3,2,1,0:T(8,128)(2,1)S(1)}, u32[]{:S(2)}, u32[]{:S(2)}) collective-permute-start(bf16[2,2,16,1536]{3,2,1,0:T(8,128)(2,1)S(1)} %bitcast.21), channel_id=1, source_target_pairs={{0,64},{32,96},{1,65},{33,97},{2,66},{34,98},{3,67},{35,99},{64,12... | collective-permute-start | bytes 589832 | tf_op jit(solution)/shard_map/gather_y/ppermute | solution.py:26
  28.1 10.6 %collective-permute-start.17 = (bf16[2,2,16,1536]{3,2,1,0:T(8,128)(2,1)S(1)}, bf16[2,2,16,1536]{3,2,1,0:T(8,128)(2,1)S(1)}, u32[]{:S(2)}, u32[]{:S(2)}) collective-permute-start(bf16[2,2,16,1536]{3,2,1,0:T(8,128)(2,1)S(1)} %bitcast.22), channel_id=1, source_target_pairs={{0,128},{32,160},{1,129},{33,161},{2,130},{34,162},{3,131},{35,163... | collective-permute-start | bytes 589832 | tf_op jit(solution)/shard_map/gather_y/ppermute | solution.py:26
  42.5 8.4 %collective-permute-start.8 = (bf16[32,1536]{1,0:T(8,128)(2,1)S(1)}, bf16[32,1536]{1,0:T(8,128)(2,1)S(1)}, u32[]{:S(2)}, u32[]{:S(2)}) collective-permute-start(bf16[32,1536]{1,0:T(8,128)(2,1)S(1)} %get-tuple-element.50), channel_id=1, source_target_pairs={{0,16},{4,20},{8,24},{12,28},{16,0},{20,4},{24,8},{28,12},{1,17},{... | collective-permute-start | bytes 294920 | tf_op jit(solution)/shard_map/reduce_x/ppermute | solution.py:31
  46.7 8.3 %collective-permute-start.20 = (bf16[32,1536]{1,0:T(8,128)(2,1)S(1)}, bf16[32,1536]{1,0:T(8,128)(2,1)S(1)}, u32[]{:S(2)}, u32[]{:S(2)}) collective-permute-start(bf16[32,1536]{1,0:T(8,128)(2,1)S(1)} %get-tuple-element.56), channel_id=1, source_target_pairs={{0,8},{4,12},{8,16},{12,20},{16,24},{20,28},{24,0},{28,4},{1,9},{5... | collective-permute-start | bytes 294920 | tf_op jit(solution)/shard_map/reduce_x/ppermute | solution.py:31
  47.4 9.9 %collective-permute-start.21 = (bf16[32,1536]{1,0:T(8,128)(2,1)S(1)}, bf16[32,1536]{1,0:T(8,128)(2,1)S(1)}, u32[]{:S(2)}, u32[]{:S(2)}) collective-permute-start(bf16[32,1536]{1,0:T(8,128)(2,1)S(1)} %get-tuple-element.57), channel_id=1, source_target_pairs={{0,16},{4,20},{8,24},{12,28},{16,0},{20,4},{24,8},{28,12},{1,17},{... | collective-permute-start | bytes 294920 | tf_op jit(solution)/shard_map/reduce_x/ppermute | solution.py:31
  48.4 9.0 %collective-permute-start.22 = (bf16[32,1536]{1,0:T(8,128)(2,1)S(1)}, bf16[32,1536]{1,0:T(8,128)(2,1)S(1)}, u32[]{:S(2)}, u32[]{:S(2)}) collective-permute-start(bf16[32,1536]{1,0:T(8,128)(2,1)S(1)} %get-tuple-element.58), channel_id=1, source_target_pairs={{0,24},{4,28},{8,0},{12,4},{16,8},{20,12},{24,16},{28,20},{1,25},{... | collective-permute-start | bytes 294920 | tf_op jit(solution)/shard_map/reduce_x/ppermute | solution.py:31
  51.7 8.3 %collective-permute-start.12 = (bf16[32,1536]{1,0:T(8,128)(2,1)S(1)}, bf16[32,1536]{1,0:T(8,128)(2,1)S(1)}, u32[]{:S(2)}, u32[]{:S(2)}) collective-permute-start(bf16[32,1536]{1,0:T(8,128)(2,1)S(1)} %get-tuple-element.52), channel_id=1, source_target_pairs={{0,8},{4,12},{8,16},{12,20},{16,24},{20,28},{24,0},{28,4},{1,9},{5... | collective-permute-start | bytes 294920 | tf_op jit(solution)/shard_map/gather_x/ppermute | solution.py:31
  52.7 8.8 %collective-permute-start.11 = (bf16[32,1536]{1,0:T(8,128)(2,1)S(1)}, bf16[32,1536]{1,0:T(8,128)(2,1)S(1)}, u32[]{:S(2)}, u32[]{:S(2)}) collective-permute-start(bf16[32,1536]{1,0:T(8,128)(2,1)S(1)} %get-tuple-element.52), channel_id=1, source_target_pairs={{0,16},{4,20},{8,24},{12,28},{16,0},{20,4},{24,8},{28,12},{1,17},{... | collective-permute-start | bytes 294920 | tf_op jit(solution)/shard_map/gather_x/ppermute | solution.py:31
  68.2 9.2 %collective-permute-start.30 = (bf16[2,2,16,1536]{3,2,1,0:T(8,128)(2,1)S(1)}, bf16[2,2,16,1536]{3,2,1,0:T(8,128)(2,1)S(1)}, u32[]{:S(2)}, u32[]{:S(2)}) collective-permute-start(bf16[2,2,16,1536]{3,2,1,0:T(8,128)(2,1)S(1)} %get-tuple-element.73), channel_id=1, source_target_pairs={{0,64},{32,96},{1,65},{33,97},{2,66},{34,98},{3,67},{35,99},{64,12... | collective-permute-start | bytes 589832 | tf_op jit(solution)/shard_map/reduce_y/ppermute | solution.py:26
  69.5 14.6 %collective-permute-start.31 = (bf16[2,2,16,1536]{3,2,1,0:T(8,128)(2,1)S(1)}, bf16[2,2,16,1536]{3,2,1,0:T(8,128)(2,1)S(1)}, u32[]{:S(2)}, u32[]{:S(2)}) collective-permute-start(bf16[2,2,16,1536]{3,2,1,0:T(8,128)(2,1)S(1)} %get-tuple-element.74), channel_id=1, source_target_pairs={{0,128},{32,160},{1,129},{33,161},{2,130},{34,162},{3,131},{35,163... | collective-permute-start | bytes 589832 | tf_op jit(solution)/shard_map/reduce_y/ppermute | solution.py:26
  72.4 11.7 %collective-permute-start.32 = (bf16[2,2,16,1536]{3,2,1,0:T(8,128)(2,1)S(1)}, bf16[2,2,16,1536]{3,2,1,0:T(8,128)(2,1)S(1)}, u32[]{:S(2)}, u32[]{:S(2)}) collective-permute-start(bf16[2,2,16,1536]{3,2,1,0:T(8,128)(2,1)S(1)} %get-tuple-element.75), channel_id=1, source_target_pairs={{0,192},{32,224},{1,193},{33,225},{2,194},{34,226},{3,195},{35,227... | collective-permute-start | bytes 589832 | tf_op jit(solution)/shard_map/reduce_y/ppermute | solution.py:26
  74.9 11.5 %collective-permute-start.27 = (bf16[2,2,16,1536]{3,2,1,0:T(8,128)(2,1)S(1)}, bf16[2,2,16,1536]{3,2,1,0:T(8,128)(2,1)S(1)}, u32[]{:S(2)}, u32[]{:S(2)}) collective-permute-start(bf16[2,2,16,1536]{3,2,1,0:T(8,128)(2,1)S(1)} %get-tuple-element.63), channel_id=1, source_target_pairs={{0,64},{32,96},{1,65},{33,97},{2,66},{34,98},{3,67},{35,99},{64,12... | collective-permute-start | bytes 589832 | tf_op jit(solution)/shard_map/reduce_y/ppermute | solution.py:26
  76.8 14.0 %collective-permute-start.28 = (bf16[2,2,16,1536]{3,2,1,0:T(8,128)(2,1)S(1)}, bf16[2,2,16,1536]{3,2,1,0:T(8,128)(2,1)S(1)}, u32[]{:S(2)}, u32[]{:S(2)}) collective-permute-start(bf16[2,2,16,1536]{3,2,1,0:T(8,128)(2,1)S(1)} %get-tuple-element.64), channel_id=1, source_target_pairs={{0,128},{32,160},{1,129},{33,161},{2,130},{34,162},{3,131},{35,163... | collective-permute-start | bytes 589832 | tf_op jit(solution)/shard_map/reduce_y/ppermute | solution.py:26
  77.4 13.3 %collective-permute-start.29 = (bf16[2,2,16,1536]{3,2,1,0:T(8,128)(2,1)S(1)}, bf16[2,2,16,1536]{3,2,1,0:T(8,128)(2,1)S(1)}, u32[]{:S(2)}, u32[]{:S(2)}) collective-permute-start(bf16[2,2,16,1536]{3,2,1,0:T(8,128)(2,1)S(1)} %get-tuple-element.65), channel_id=1, source_target_pairs={{0,192},{32,224},{1,193},{33,225},{2,194},{34,226},{3,195},{35,227... | collective-permute-start | bytes 589832 | tf_op jit(solution)/shard_map/reduce_y/ppermute | solution.py:26
  84.2 10.0 %collective-permute-start.33 = (bf16[16,1536]{1,0:T(8,128)(2,1)S(1)}, bf16[16,1536]{1,0:T(8,128)(2,1)S(1)}, u32[]{:S(2)}, u32[]{:S(2)}) collective-permute-start(bf16[16,1536]{1,0:T(8,128)(2,1)S(1)} %get-tuple-element.78), channel_id=1, source_target_pairs={{0,32},{32,0},{1,33},{33,1},{2,34},{34,2},{3,35},{35,3},{64,96},{9... | collective-permute-start | bytes 147464 | tf_op jit(solution)/shard_map/reduce_z/ppermute | solution.py:26
  84.8 12.0 %collective-permute-start.36 = (bf16[16,1536]{1,0:T(8,128)(2,1)S(1)}, bf16[16,1536]{1,0:T(8,128)(2,1)S(1)}, u32[]{:S(2)}, u32[]{:S(2)}) collective-permute-start(bf16[16,1536]{1,0:T(8,128)(2,1)S(1)} %get-tuple-element.80), channel_id=1, source_target_pairs={{0,2},{32,34},{1,3},{33,35},{2,0},{34,32},{3,1},{35,33},{64,66},{9... | collective-permute-start | bytes 147464 | tf_op jit(solution)/shard_map/reduce_z/ppermute | solution.py:26
  86.4 14.6 %collective-permute-start.37 = (bf16[16,1536]{1,0:T(8,128)(2,1)S(1)}, bf16[16,1536]{1,0:T(8,128)(2,1)S(1)}, u32[]{:S(2)}, u32[]{:S(2)}) collective-permute-start(bf16[16,1536]{1,0:T(8,128)(2,1)S(1)} %get-tuple-element.81), channel_id=1, source_target_pairs={{0,34},{32,2},{1,35},{33,3},{2,32},{34,0},{3,33},{35,1},{64,98},{9... | collective-permute-start | bytes 147464 | tf_op jit(solution)/shard_map/reduce_z/ppermute | solution.py:26
  90.9 10.1 %collective-permute-start.35 = (bf16[16,1536]{1,0:T(8,128)(2,1)S(1)}, bf16[16,1536]{1,0:T(8,128)(2,1)S(1)}, u32[]{:S(2)}, u32[]{:S(2)}) collective-permute-start(bf16[16,1536]{1,0:T(8,128)(2,1)S(1)} %get-tuple-element.79), channel_id=1, source_target_pairs={{0,33},{32,1},{1,34},{33,2},{2,35},{34,3},{3,32},{35,0},{64,97},{9... | collective-permute-start | bytes 147464 | tf_op jit(solution)/shard_map/reduce_z/ppermute | solution.py:26
  91.0 10.0 %collective-permute-start.38 = (bf16[16,1536]{1,0:T(8,128)(2,1)S(1)}, bf16[16,1536]{1,0:T(8,128)(2,1)S(1)}, u32[]{:S(2)}, u32[]{:S(2)}) collective-permute-start(bf16[16,1536]{1,0:T(8,128)(2,1)S(1)} %get-tuple-element.82), channel_id=1, source_target_pairs={{0,3},{32,35},{1,0},{33,32},{2,1},{34,33},{3,2},{35,34},{64,67},{9... | collective-permute-start | bytes 147464 | tf_op jit(solution)/shard_map/reduce_z/ppermute | solution.py:26
  (18 other events, 133.0 us)

commit v4 on v3

--- a/solution.py
+++ b/solution.py
@@ -232,12 +232,10 @@
     width = grads[0].shape[2]
 
     def body(place, *refs):
-        total = jnp.zeros((1, width), F32)
-        for ref in refs[: len(grads)]:
-            part = ref[...].reshape(-1, width).astype(F32)
-            total = total + jnp.sum(part, axis=0, keepdims=True)
+        rows = jnp.concatenate([ref[...].reshape(-1, width) for ref in refs[: len(grads)]])
+        ones = jnp.ones((ROW, rows.shape[0]), BF)
         bias, act = refs[-2:]
-        bias[...] = total
+        bias[...] = jnp.dot(ones, rows, preferred_element_type=F32)[:1]
         for chunk, ref in zip(CHUNKS, refs[len(grads) : -2]):
             for j, e in enumerate(chunk):
                 act[(place[4] + e) & 3] = ref[j * ROW : (j + 1) * ROW, :]

time: 104 us -> 104 us (level)
  transfers between devices with their start and end apart: 40 -> 40, of which waited for: 10 -> 10; matrix products, arithmetic and copies ran while one was open for 1% -> 1% of each run, Pallas kernels for 17% -> 18%
where the time goes in v4:
time: 104 us
  starting transfers between devices  64 us (62%)
  waiting for transfers between devices  19.2 us (18%)
  Pallas kernels  18.9 us (18%)
    ppermute x24, starting transfers between devices, by_plane(): return lax.ppermute(array, PLANE, pairs)  45.4 us
    pallas_call x16, Pallas kernels, call(): pl.pallas_call(run, grid=grid, in_specs=in_specs, out_specs=out_specs or...  18.9 us
    ppermute x16, starting transfers between devices, by_line(): return lax.ppermute(array, 'gy', pairs)  18.6 us
    ppermute x24, waiting for transfers between devices, by_plane(): return lax.ppermute(array, PLANE, pairs)  14.2 us
    ppermute x16, waiting for transfers between devices, by_line(): return lax.ppermute(array, 'gy', pairs)  5.06 us
  transfers between devices with their start and end apart: 40, of which 10 were waited for; matrix products, arithmetic and copies ran while one was open for 1% of the time, Pallas kernels for 18%

profile of v4, /device:TPU:32, one launch (start us, length us, event | category | flops | bytes accessed | tf_op | source)
XLA Modules:
  0.0 103.9 jit_solution(6153837393162289994)
XLA Ops:
  0.6 1.9 %collective-permute-start = (bf16[16,1536]{1,0:T(8,128)(2,1)}, bf16[16,1536]{1,0:T(8,128)(2,1)S(1)}, u32[]{:S(2)}, u32[]{:S(2)}) collective-permute-start(bf16[16,1536]{1,0:T(8,128)(2,1)} %refs_1_.1), channel_id=1, source_target_pairs={{0,32},{32,0},{1,33},{33,1},{2,34},{34,2},{3,35},{35,3},{64,96},{9... | collective-permute-start | bytes 147464 | tf_op jit(solution)/shard_map/gather_z/ppermute | solution.py:26
  2.6 5.0 %collective-permute-start.2 = (bf16[16,1536]{1,0:T(8,128)(2,1)}, bf16[16,1536]{1,0:T(8,128)(2,1)S(1)}, u32[]{:S(2)}, u32[]{:S(2)}) collective-permute-start(bf16[16,1536]{1,0:T(8,128)(2,1)} %refs_1_.1), channel_id=1, source_target_pairs={{0,34},{32,2},{1,35},{33,3},{2,32},{34,0},{3,33},{35,1},{64,98},{9... | collective-permute-start | bytes 147464 | tf_op jit(solution)/shard_map/gather_z/ppermute | solution.py:26
  8.1 2.4 %gather_z.3 = (bf16[1536,1536]{1,0:T(8,128)(2,1)S(1)}, bf16[16,1536]{1,0:T(8,128)(2,1)S(1)}) custom-call(bf16[1536,1536]{1,0:T(8,128)(2,1)} %refs_0_.1, bf16[16,1536]{1,0:T(8,128)(2,1)} %refs_1_.1, s32[5]{0:T(128)S(1)} %stack.53.refs_2_.refs_0_), custom_call_target="tpu_custom_call" | custom-call | tf_op jit(solution)/shard_map/gather_z/pallas_call | solution.py:45
  10.5 6.0 %collective-permute-done.1.refs_2_ = bf16[16,1536]{1,0:T(8,128)(2,1)S(1)} collective-permute-done((bf16[16,1536]{1,0:T(8,128)(2,1)}, bf16[16,1536]{1,0:T(8,128)(2,1)S(1)}, u32[]{:S(2)}, u32[]{:S(2)}) %collective-permute-start.1) | collective-permute-done | bytes 49184 | tf_op jit(solution)/shard_map/gather_z/ppermute | solution.py:26
  21.2 2.8 %collective-permute-start.14 = (bf16[2,16,1536]{2,1,0:T(8,128)(2,1)S(1)}, bf16[2,16,1536]{2,1,0:T(8,128)(2,1)S(1)}, u32[]{:S(2)}, u32[]{:S(2)}) collective-permute-start(bf16[2,16,1536]{2,1,0:T(8,128)(2,1)S(1)} %slice.4), channel_id=1, source_target_pairs={{0,3},{32,35},{1,0},{33,32},{2,1},{34,33},{3,2},{35,34},{64,67},{9... | collective-permute-start | bytes 294920 | tf_op jit(solution)/shard_map/gather_z/ppermute | solution.py:26
  24.0 2.0 %collective-permute-start.4 = (bf16[2,2,16,1536]{3,2,1,0:T(8,128)(2,1)S(1)}, bf16[2,2,16,1536]{3,2,1,0:T(8,128)(2,1)S(1)}, u32[]{:S(2)}, u32[]{:S(2)}) collective-permute-start(bf16[2,2,16,1536]{3,2,1,0:T(8,128)(2,1)S(1)} %bitcast.19), channel_id=1, source_target_pairs={{0,128},{32,160},{1,129},{33,161},{2,130},{34,162},{3,131},{35,163... | collective-permute-start | bytes 589832 | tf_op jit(solution)/shard_map/gather_y/ppermute | solution.py:26
  28.1 2.9 %collective-permute-start.17 = (bf16[2,2,16,1536]{3,2,1,0:T(8,128)(2,1)S(1)}, bf16[2,2,16,1536]{3,2,1,0:T(8,128)(2,1)S(1)}, u32[]{:S(2)}, u32[]{:S(2)}) collective-permute-start(bf16[2,2,16,1536]{3,2,1,0:T(8,128)(2,1)S(1)} %bitcast.22), channel_id=1, source_target_pairs={{0,128},{32,160},{1,129},{33,161},{2,130},{34,162},{3,131},{35,163... | collective-permute-start | bytes 589832 | tf_op jit(solution)/shard_map/gather_y/ppermute | solution.py:26
  33.3 1.9 %project.2 = (bf16[2,4,2,16,1536]{4,3,2,1,0:T(8,128)(2,1)S(1)}, f32[4,32,1536]{2,1,0:T(8,128)S(1)}, bf16[4,32,1536]{2,1,0:T(8,128)(2,1)S(1)}) custom-call(s32[5]{0:T(128)S(1)} %stack.53.refs_2_.refs_0_, bf16[2,2,16,1536]{3,2,1,0:T(8,128)(2,1)S(1)} %bitcast.20, bf16[2,2,16,1536]{3,2,1,0:T(8,128)(2,1)S(1)} %collective-permute-done.3.refs_2_, ...), custom_call_target="tpu_custom_call" | custom-call | tf_op jit(solution)/shard_map/project/pallas_call | solution.py:45
  36.6 2.1 %collective-permute-done.17.refs_3_ = bf16[2,2,16,1536]{3,2,1,0:T(8,128)(2,1)S(1)} collective-permute-done((bf16[2,2,16,1536]{3,2,1,0:T(8,128)(2,1)S(1)}, bf16[2,2,16,1536]{3,2,1,0:T(8,128)(2,1)S(1)}, u32[]{:S(2)}, u32[]{:S(2)}) %collective-permute-start.17) | collective-permute-done | bytes 196640 | tf_op jit(solution)/shard_map/gather_y/ppermute | solution.py:26
  38.8 1.9 %project.3 = (bf16[2,4,2,16,1536]{4,3,2,1,0:T(8,128)(2,1)S(1)}, f32[4,32,1536]{2,1,0:T(8,128)S(1)}, bf16[4,32,1536]{2,1,0:T(8,128)(2,1)S(1)}) custom-call(s32[5]{0:T(128)S(1)} %stack.53.refs_2_.refs_0_, bf16[2,2,16,1536]{3,2,1,0:T(8,128)(2,1)S(1)} %bitcast.24, bf16[2,2,16,1536]{3,2,1,0:T(8,128)(2,1)S(1)} %collective-permute-done.16.refs_2_, ...), custom_call_target="tpu_custom_call" | custom-call | tf_op jit(solution)/shard_map/project/pallas_call | solution.py:45
  42.5 2.7 %collective-permute-start.8 = (bf16[32,1536]{1,0:T(8,128)(2,1)S(1)}, bf16[32,1536]{1,0:T(8,128)(2,1)S(1)}, u32[]{:S(2)}, u32[]{:S(2)}) collective-permute-start(bf16[32,1536]{1,0:T(8,128)(2,1)S(1)} %get-tuple-element.50), channel_id=1, source_target_pairs={{0,16},{4,20},{8,24},{12,28},{16,0},{20,4},{24,8},{28,12},{1,17},{... | collective-permute-start | bytes 294920 | tf_op jit(solution)/shard_map/reduce_x/ppermute | solution.py:31
  52.7 2.4 %collective-permute-start.11 = (bf16[32,1536]{1,0:T(8,128)(2,1)S(1)}, bf16[32,1536]{1,0:T(8,128)(2,1)S(1)}, u32[]{:S(2)}, u32[]{:S(2)}) collective-permute-start(bf16[32,1536]{1,0:T(8,128)(2,1)S(1)} %get-tuple-element.52), channel_id=1, source_target_pairs={{0,16},{4,20},{8,24},{12,28},{16,0},{20,4},{24,8},{28,12},{1,17},{... | collective-permute-start | bytes 294920 | tf_op jit(solution)/shard_map/gather_x/ppermute | solution.py:31
  55.0 2.3 %collective-permute-start.10 = (bf16[32,1536]{1,0:T(8,128)(2,1)S(1)}, bf16[32,1536]{1,0:T(8,128)(2,1)S(1)}, u32[]{:S(2)}, u32[]{:S(2)}) collective-permute-start(bf16[32,1536]{1,0:T(8,128)(2,1)S(1)} %get-tuple-element.52), channel_id=1, source_target_pairs={{0,24},{4,28},{8,0},{12,4},{16,8},{20,12},{24,16},{28,20},{1,25},{... | collective-permute-start | bytes 294920 | tf_op jit(solution)/shard_map/gather_x/ppermute | solution.py:31
  61.6 3.5 %collective-permute-done.25 = bf16[32,1536]{1,0:T(8,128)(2,1)S(1)} collective-permute-done((bf16[32,1536]{1,0:T(8,128)(2,1)S(1)}, bf16[32,1536]{1,0:T(8,128)(2,1)S(1)}, u32[]{:S(2)}, u32[]{:S(2)}) %collective-permute-start.25) | collective-permute-done | bytes 98336 | tf_op jit(solution)/shard_map/gather_x/ppermute | solution.py:31
  66.1 2.1 %back.3 = (f32[2,2,16,1536]{3,2,1,0:T(8,128)S(1)}, bf16[2,2,16,1536]{3,2,1,0:T(8,128)(2,1)S(1)}, bf16[2,2,16,1536]{3,2,1,0:T(8,128)(2,1)S(1)}, bf16[2,2,16,1536]{3,2,1,0:T(8,128)(2,1)S(1)}) custom-call(s32[5]{0:T(128)S(1)} %stack.53.refs_2_.refs_0_, bf16[4,32,1536]{2,1,0:T(8,128)(2,1)S(1)} %pad_maximum_fusion.refs_1_.refs_2_, ...), custom_call_target="tpu_custom_call" | custom-call | tf_op jit(solution)/shard_map/back/pallas_call | solution.py:45
  69.5 2.9 %collective-permute-start.31 = (bf16[2,2,16,1536]{3,2,1,0:T(8,128)(2,1)S(1)}, bf16[2,2,16,1536]{3,2,1,0:T(8,128)(2,1)S(1)}, u32[]{:S(2)}, u32[]{:S(2)}) collective-permute-start(bf16[2,2,16,1536]{3,2,1,0:T(8,128)(2,1)S(1)} %get-tuple-element.74), channel_id=1, source_target_pairs={{0,128},{32,160},{1,129},{33,161},{2,130},{34,162},{3,131},{35,163... | collective-permute-start | bytes 589832 | tf_op jit(solution)/shard_map/reduce_y/ppermute | solution.py:26
  72.8 2.1 %back.2 = (f32[2,2,16,1536]{3,2,1,0:T(8,128)S(1)}, bf16[2,2,16,1536]{3,2,1,0:T(8,128)(2,1)S(1)}, bf16[2,2,16,1536]{3,2,1,0:T(8,128)(2,1)S(1)}, bf16[2,2,16,1536]{3,2,1,0:T(8,128)(2,1)S(1)}) custom-call(s32[5]{0:T(128)S(1)} %stack.53.refs_2_.refs_0_, bf16[4,32,1536]{2,1,0:T(8,128)(2,1)S(1)} %pad_maximum_fusion.1.refs_1_.refs_3_.refs_4_, ...), custom_call_target="tpu_custom_call" | custom-call | tf_op jit(solution)/shard_map/back/pallas_call | solution.py:45
  77.4 2.1 %collective-permute-start.29 = (bf16[2,2,16,1536]{3,2,1,0:T(8,128)(2,1)S(1)}, bf16[2,2,16,1536]{3,2,1,0:T(8,128)(2,1)S(1)}, u32[]{:S(2)}, u32[]{:S(2)}) collective-permute-start(bf16[2,2,16,1536]{3,2,1,0:T(8,128)(2,1)S(1)} %get-tuple-element.65), channel_id=1, source_target_pairs={{0,192},{32,224},{1,193},{33,225},{2,194},{34,226},{3,195},{35,227... | collective-permute-start | bytes 589832 | tf_op jit(solution)/shard_map/reduce_y/ppermute | solution.py:26
  79.6 4.5 %weigh.1 = (bf16[1536,1536]{1,0:T(8,128)(2,1)}, f32[8,128]{1,0:T(8,128)S(1)}) custom-call(bf16[2,4,2,16,1536]{4,3,2,1,0:T(8,128)(2,1)S(1)} %get-tuple-element.69.refs_0_, bf16[2,4,2,16,1536]{4,3,2,1,0:T(8,128)(2,1)S(1)} %get-tuple-element.70.refs_1_, bf16[4,32,1536]{2,1,0:T(8,128)(2,1)S(1)} %pad_maximum_fusion.refs_1_.refs_2_, ...), custom_call_target="tpu_custom_call" | custom-call | tf_op jit(solution)/shard_map/weigh/pallas_call | solution.py:45
  86.4 4.4 %collective-permute-start.37 = (bf16[16,1536]{1,0:T(8,128)(2,1)S(1)}, bf16[16,1536]{1,0:T(8,128)(2,1)S(1)}, u32[]{:S(2)}, u32[]{:S(2)}) collective-permute-start(bf16[16,1536]{1,0:T(8,128)(2,1)S(1)} %get-tuple-element.81), channel_id=1, source_target_pairs={{0,34},{32,2},{1,35},{33,3},{2,32},{34,0},{3,33},{35,1},{64,98},{9... | collective-permute-start | bytes 147464 | tf_op jit(solution)/shard_map/reduce_z/ppermute | solution.py:26
  91.0 3.2 %collective-permute-start.38 = (bf16[16,1536]{1,0:T(8,128)(2,1)S(1)}, bf16[16,1536]{1,0:T(8,128)(2,1)S(1)}, u32[]{:S(2)}, u32[]{:S(2)}) collective-permute-start(bf16[16,1536]{1,0:T(8,128)(2,1)S(1)} %get-tuple-element.82), channel_id=1, source_target_pairs={{0,3},{32,35},{1,0},{33,32},{2,1},{34,33},{3,2},{35,34},{64,67},{9... | collective-permute-start | bytes 147464 | tf_op jit(solution)/shard_map/reduce_z/ppermute | solution.py:26
  94.2 2.7 %collective-permute-start.39 = (bf16[16,1536]{1,0:T(8,128)(2,1)S(1)}, bf16[16,1536]{1,0:T(8,128)(2,1)S(1)}, u32[]{:S(2)}, u32[]{:S(2)}) collective-permute-start(bf16[16,1536]{1,0:T(8,128)(2,1)S(1)} %get-tuple-element.83), channel_id=1, source_target_pairs={{0,35},{32,3},{1,32},{33,0},{2,33},{34,1},{3,34},{35,2},{64,99},{9... | collective-permute-start | bytes 147464 | tf_op jit(solution)/shard_map/reduce_z/ppermute | solution.py:26
  96.8 2.1 %collective-permute-start.34 = (bf16[16,1536]{1,0:T(8,128)(2,1)S(1)}, bf16[16,1536]{1,0:T(8,128)(2,1)S(1)}, u32[]{:S(2)}, u32[]{:S(2)}) collective-permute-start(bf16[16,1536]{1,0:T(8,128)(2,1)S(1)} %get-tuple-element.66.refs_7_), channel_id=1, source_target_pairs={{0,1},{32,33},{1,2},{33,34},{2,3},{34,35},{3,0},{35,32},{64,65},{9... | collective-permute-start | bytes 147464 | tf_op jit(solution)/shard_map/reduce_z/ppermute | solution.py:26
  101.0 2.1 %collective-permute-done.34.refs_2_ = bf16[16,1536]{1,0:T(8,128)(2,1)S(1)} collective-permute-done((bf16[16,1536]{1,0:T(8,128)(2,1)S(1)}, bf16[16,1536]{1,0:T(8,128)(2,1)S(1)}, u32[]{:S(2)}, u32[]{:S(2)}) %collective-permute-start.34) | collective-permute-done | bytes 49184 | tf_op jit(solution)/shard_map/reduce_z/ppermute | solution.py:26
  (82 shorter events, 35.1 us)
Async XLA Ops:
  0.6 9.8 %collective-permute-start = (bf16[16,1536]{1,0:T(8,128)(2,1)}, bf16[16,1536]{1,0:T(8,128)(2,1)S(1)}, u32[]{:S(2)}, u32[]{:S(2)}) collective-permute-start(bf16[16,1536]{1,0:T(8,128)(2,1)} %refs_1_.1), channel_id=1, source_target_pairs={{0,32},{32,0},{1,33},{33,1},{2,34},{34,2},{3,35},{35,3},{64,96},{9... | collective-permute-start | bytes 147464 | tf_op jit(solution)/shard_map/gather_z/ppermute | solution.py:26
  7.6 8.9 %collective-permute-start.1 = (bf16[16,1536]{1,0:T(8,128)(2,1)}, bf16[16,1536]{1,0:T(8,128)(2,1)S(1)}, u32[]{:S(2)}, u32[]{:S(2)}) collective-permute-start(bf16[16,1536]{1,0:T(8,128)(2,1)} %refs_1_.1), channel_id=1, source_target_pairs={{0,2},{32,34},{1,3},{33,35},{2,0},{34,32},{3,1},{35,33},{64,66},{9... | collective-permute-start | bytes 147464 | tf_op jit(solution)/shard_map/gather_z/ppermute | solution.py:26
  16.5 11.1 %collective-permute-start.5 = (bf16[2,2,16,1536]{3,2,1,0:T(8,128)(2,1)S(1)}, bf16[2,2,16,1536]{3,2,1,0:T(8,128)(2,1)S(1)}, u32[]{:S(2)}, u32[]{:S(2)}) collective-permute-start(bf16[2,2,16,1536]{3,2,1,0:T(8,128)(2,1)S(1)} %bitcast.17), channel_id=1, source_target_pairs={{0,64},{32,96},{1,65},{33,97},{2,66},{34,98},{3,67},{35,99},{64,12... | collective-permute-start | bytes 589832 | tf_op jit(solution)/shard_map/gather_y/ppermute | solution.py:26
  18.1 9.5 %collective-permute-start.3 = (bf16[2,2,16,1536]{3,2,1,0:T(8,128)(2,1)S(1)}, bf16[2,2,16,1536]{3,2,1,0:T(8,128)(2,1)S(1)}, u32[]{:S(2)}, u32[]{:S(2)}) collective-permute-start(bf16[2,2,16,1536]{3,2,1,0:T(8,128)(2,1)S(1)} %bitcast.18), channel_id=1, source_target_pairs={{0,192},{32,224},{1,193},{33,225},{2,194},{34,226},{3,195},{35,227... | collective-permute-start | bytes 589832 | tf_op jit(solution)/shard_map/gather_y/ppermute | solution.py:26
  24.0 9.3 %collective-permute-start.4 = (bf16[2,2,16,1536]{3,2,1,0:T(8,128)(2,1)S(1)}, bf16[2,2,16,1536]{3,2,1,0:T(8,128)(2,1)S(1)}, u32[]{:S(2)}, u32[]{:S(2)}) collective-permute-start(bf16[2,2,16,1536]{3,2,1,0:T(8,128)(2,1)S(1)} %bitcast.19), channel_id=1, source_target_pairs={{0,128},{32,160},{1,129},{33,161},{2,130},{34,162},{3,131},{35,163... | collective-permute-start | bytes 589832 | tf_op jit(solution)/shard_map/gather_y/ppermute | solution.py:26
  27.6 9.0 %collective-permute-start.18 = (bf16[2,2,16,1536]{3,2,1,0:T(8,128)(2,1)S(1)}, bf16[2,2,16,1536]{3,2,1,0:T(8,128)(2,1)S(1)}, u32[]{:S(2)}, u32[]{:S(2)}) collective-permute-start(bf16[2,2,16,1536]{3,2,1,0:T(8,128)(2,1)S(1)} %bitcast.21), channel_id=1, source_target_pairs={{0,64},{32,96},{1,65},{33,97},{2,66},{34,98},{3,67},{35,99},{64,12... | collective-permute-start | bytes 589832 | tf_op jit(solution)/shard_map/gather_y/ppermute | solution.py:26
  28.1 10.6 %collective-permute-start.17 = (bf16[2,2,16,1536]{3,2,1,0:T(8,128)(2,1)S(1)}, bf16[2,2,16,1536]{3,2,1,0:T(8,128)(2,1)S(1)}, u32[]{:S(2)}, u32[]{:S(2)}) collective-permute-start(bf16[2,2,16,1536]{3,2,1,0:T(8,128)(2,1)S(1)} %bitcast.22), channel_id=1, source_target_pairs={{0,128},{32,160},{1,129},{33,161},{2,130},{34,162},{3,131},{35,163... | collective-permute-start | bytes 589832 | tf_op jit(solution)/shard_map/gather_y/ppermute | solution.py:26
  42.5 8.4 %collective-permute-start.8 = (bf16[32,1536]{1,0:T(8,128)(2,1)S(1)}, bf16[32,1536]{1,0:T(8,128)(2,1)S(1)}, u32[]{:S(2)}, u32[]{:S(2)}) collective-permute-start(bf16[32,1536]{1,0:T(8,128)(2,1)S(1)} %get-tuple-element.50), channel_id=1, source_target_pairs={{0,16},{4,20},{8,24},{12,28},{16,0},{20,4},{24,8},{28,12},{1,17},{... | collective-permute-start | bytes 294920 | tf_op jit(solution)/shard_map/reduce_x/ppermute | solution.py:31
  46.7 8.3 %collective-permute-start.20 = (bf16[32,1536]{1,0:T(8,128)(2,1)S(1)}, bf16[32,1536]{1,0:T(8,128)(2,1)S(1)}, u32[]{:S(2)}, u32[]{:S(2)}) collective-permute-start(bf16[32,1536]{1,0:T(8,128)(2,1)S(1)} %get-tuple-element.56), channel_id=1, source_target_pairs={{0,8},{4,12},{8,16},{12,20},{16,24},{20,28},{24,0},{28,4},{1,9},{5... | collective-permute-start | bytes 294920 | tf_op jit(solution)/shard_map/reduce_x/ppermute | solution.py:31
  47.4 9.9 %collective-permute-start.21 = (bf16[32,1536]{1,0:T(8,128)(2,1)S(1)}, bf16[32,1536]{1,0:T(8,128)(2,1)S(1)}, u32[]{:S(2)}, u32[]{:S(2)}) collective-permute-start(bf16[32,1536]{1,0:T(8,128)(2,1)S(1)} %get-tuple-element.57), channel_id=1, source_target_pairs={{0,16},{4,20},{8,24},{12,28},{16,0},{20,4},{24,8},{28,12},{1,17},{... | collective-permute-start | bytes 294920 | tf_op jit(solution)/shard_map/reduce_x/ppermute | solution.py:31
  48.4 9.0 %collective-permute-start.22 = (bf16[32,1536]{1,0:T(8,128)(2,1)S(1)}, bf16[32,1536]{1,0:T(8,128)(2,1)S(1)}, u32[]{:S(2)}, u32[]{:S(2)}) collective-permute-start(bf16[32,1536]{1,0:T(8,128)(2,1)S(1)} %get-tuple-element.58), channel_id=1, source_target_pairs={{0,24},{4,28},{8,0},{12,4},{16,8},{20,12},{24,16},{28,20},{1,25},{... | collective-permute-start | bytes 294920 | tf_op jit(solution)/shard_map/reduce_x/ppermute | solution.py:31
  51.7 8.3 %collective-permute-start.12 = (bf16[32,1536]{1,0:T(8,128)(2,1)S(1)}, bf16[32,1536]{1,0:T(8,128)(2,1)S(1)}, u32[]{:S(2)}, u32[]{:S(2)}) collective-permute-start(bf16[32,1536]{1,0:T(8,128)(2,1)S(1)} %get-tuple-element.52), channel_id=1, source_target_pairs={{0,8},{4,12},{8,16},{12,20},{16,24},{20,28},{24,0},{28,4},{1,9},{5... | collective-permute-start | bytes 294920 | tf_op jit(solution)/shard_map/gather_x/ppermute | solution.py:31
  52.7 8.8 %collective-permute-start.11 = (bf16[32,1536]{1,0:T(8,128)(2,1)S(1)}, bf16[32,1536]{1,0:T(8,128)(2,1)S(1)}, u32[]{:S(2)}, u32[]{:S(2)}) collective-permute-start(bf16[32,1536]{1,0:T(8,128)(2,1)S(1)} %get-tuple-element.52), channel_id=1, source_target_pairs={{0,16},{4,20},{8,24},{12,28},{16,0},{20,4},{24,8},{28,12},{1,17},{... | collective-permute-start | bytes 294920 | tf_op jit(solution)/shard_map/gather_x/ppermute | solution.py:31
  68.2 9.2 %collective-permute-start.30 = (bf16[2,2,16,1536]{3,2,1,0:T(8,128)(2,1)S(1)}, bf16[2,2,16,1536]{3,2,1,0:T(8,128)(2,1)S(1)}, u32[]{:S(2)}, u32[]{:S(2)}) collective-permute-start(bf16[2,2,16,1536]{3,2,1,0:T(8,128)(2,1)S(1)} %get-tuple-element.73), channel_id=1, source_target_pairs={{0,64},{32,96},{1,65},{33,97},{2,66},{34,98},{3,67},{35,99},{64,12... | collective-permute-start | bytes 589832 | tf_op jit(solution)/shard_map/reduce_y/ppermute | solution.py:26
  69.5 14.6 %collective-permute-start.31 = (bf16[2,2,16,1536]{3,2,1,0:T(8,128)(2,1)S(1)}, bf16[2,2,16,1536]{3,2,1,0:T(8,128)(2,1)S(1)}, u32[]{:S(2)}, u32[]{:S(2)}) collective-permute-start(bf16[2,2,16,1536]{3,2,1,0:T(8,128)(2,1)S(1)} %get-tuple-element.74), channel_id=1, source_target_pairs={{0,128},{32,160},{1,129},{33,161},{2,130},{34,162},{3,131},{35,163... | collective-permute-start | bytes 589832 | tf_op jit(solution)/shard_map/reduce_y/ppermute | solution.py:26
  72.4 11.7 %collective-permute-start.32 = (bf16[2,2,16,1536]{3,2,1,0:T(8,128)(2,1)S(1)}, bf16[2,2,16,1536]{3,2,1,0:T(8,128)(2,1)S(1)}, u32[]{:S(2)}, u32[]{:S(2)}) collective-permute-start(bf16[2,2,16,1536]{3,2,1,0:T(8,128)(2,1)S(1)} %get-tuple-element.75), channel_id=1, source_target_pairs={{0,192},{32,224},{1,193},{33,225},{2,194},{34,226},{3,195},{35,227... | collective-permute-start | bytes 589832 | tf_op jit(solution)/shard_map/reduce_y/ppermute | solution.py:26
  74.9 11.5 %collective-permute-start.27 = (bf16[2,2,16,1536]{3,2,1,0:T(8,128)(2,1)S(1)}, bf16[2,2,16,1536]{3,2,1,0:T(8,128)(2,1)S(1)}, u32[]{:S(2)}, u32[]{:S(2)}) collective-permute-start(bf16[2,2,16,1536]{3,2,1,0:T(8,128)(2,1)S(1)} %get-tuple-element.63), channel_id=1, source_target_pairs={{0,64},{32,96},{1,65},{33,97},{2,66},{34,98},{3,67},{35,99},{64,12... | collective-permute-start | bytes 589832 | tf_op jit(solution)/shard_map/reduce_y/ppermute | solution.py:26
  76.8 14.0 %collective-permute-start.28 = (bf16[2,2,16,1536]{3,2,1,0:T(8,128)(2,1)S(1)}, bf16[2,2,16,1536]{3,2,1,0:T(8,128)(2,1)S(1)}, u32[]{:S(2)}, u32[]{:S(2)}) collective-permute-start(bf16[2,2,16,1536]{3,2,1,0:T(8,128)(2,1)S(1)} %get-tuple-element.64), channel_id=1, source_target_pairs={{0,128},{32,160},{1,129},{33,161},{2,130},{34,162},{3,131},{35,163... | collective-permute-start | bytes 589832 | tf_op jit(solution)/shard_map/reduce_y/ppermute | solution.py:26
  77.4 13.3 %collective-permute-start.29 = (bf16[2,2,16,1536]{3,2,1,0:T(8,128)(2,1)S(1)}, bf16[2,2,16,1536]{3,2,1,0:T(8,128)(2,1)S(1)}, u32[]{:S(2)}, u32[]{:S(2)}) collective-permute-start(bf16[2,2,16,1536]{3,2,1,0:T(8,128)(2,1)S(1)} %get-tuple-element.65), channel_id=1, source_target_pairs={{0,192},{32,224},{1,193},{33,225},{2,194},{34,226},{3,195},{35,227... | collective-permute-start | bytes 589832 | tf_op jit(solution)/shard_map/reduce_y/ppermute | solution.py:26
  84.2 10.0 %collective-permute-start.33 = (bf16[16,1536]{1,0:T(8,128)(2,1)S(1)}, bf16[16,1536]{1,0:T(8,128)(2,1)S(1)}, u32[]{:S(2)}, u32[]{:S(2)}) collective-permute-start(bf16[16,1536]{1,0:T(8,128)(2,1)S(1)} %get-tuple-element.78), channel_id=1, source_target_pairs={{0,32},{32,0},{1,33},{33,1},{2,34},{34,2},{3,35},{35,3},{64,96},{9... | collective-permute-start | bytes 147464 | tf_op jit(solution)/shard_map/reduce_z/ppermute | solution.py:26
  84.8 12.0 %collective-permute-start.36 = (bf16[16,1536]{1,0:T(8,128)(2,1)S(1)}, bf16[16,1536]{1,0:T(8,128)(2,1)S(1)}, u32[]{:S(2)}, u32[]{:S(2)}) collective-permute-start(bf16[16,1536]{1,0:T(8,128)(2,1)S(1)} %get-tuple-element.80), channel_id=1, source_target_pairs={{0,2},{32,34},{1,3},{33,35},{2,0},{34,32},{3,1},{35,33},{64,66},{9... | collective-permute-start | bytes 147464 | tf_op jit(solution)/shard_map/reduce_z/ppermute | solution.py:26
  86.4 14.6 %collective-permute-start.37 = (bf16[16,1536]{1,0:T(8,128)(2,1)S(1)}, bf16[16,1536]{1,0:T(8,128)(2,1)S(1)}, u32[]{:S(2)}, u32[]{:S(2)}) collective-permute-start(bf16[16,1536]{1,0:T(8,128)(2,1)S(1)} %get-tuple-element.81), channel_id=1, source_target_pairs={{0,34},{32,2},{1,35},{33,3},{2,32},{34,0},{3,33},{35,1},{64,98},{9... | collective-permute-start | bytes 147464 | tf_op jit(solution)/shard_map/reduce_z/ppermute | solution.py:26
  90.9 10.1 %collective-permute-start.35 = (bf16[16,1536]{1,0:T(8,128)(2,1)S(1)}, bf16[16,1536]{1,0:T(8,128)(2,1)S(1)}, u32[]{:S(2)}, u32[]{:S(2)}) collective-permute-start(bf16[16,1536]{1,0:T(8,128)(2,1)S(1)} %get-tuple-element.79), channel_id=1, source_target_pairs={{0,33},{32,1},{1,34},{33,2},{2,35},{34,3},{3,32},{35,0},{64,97},{9... | collective-permute-start | bytes 147464 | tf_op jit(solution)/shard_map/reduce_z/ppermute | solution.py:26
  91.0 10.0 %collective-permute-start.38 = (bf16[16,1536]{1,0:T(8,128)(2,1)S(1)}, bf16[16,1536]{1,0:T(8,128)(2,1)S(1)}, u32[]{:S(2)}, u32[]{:S(2)}) collective-permute-start(bf16[16,1536]{1,0:T(8,128)(2,1)S(1)} %get-tuple-element.82), channel_id=1, source_target_pairs={{0,3},{32,35},{1,0},{33,32},{2,1},{34,33},{3,2},{35,34},{64,67},{9... | collective-permute-start | bytes 147464 | tf_op jit(solution)/shard_map/reduce_z/ppermute | solution.py:26
  (18 other events, 133.1 us)
